TPU v7x, 512 devices: a whole 4x4x16 slice. The times are simulated.
512 devices in a mesh: ctx: 16 (over z), head: 32 (over y, x, core).
Axes of the slice: x: 4, y: 4, z: 16, core: 2. Of those that a mesh axis runs over, the one named last changes fastest.
Arguments:
- queries: bfloat16 [16384, 8192], P(('ctx', 'head')), may hold values from -12 to 12
- key_state_rows: bfloat16 [16384, 1024], P(('ctx', 'head')), may hold values from -3.5 to 3.5
- value_state_rows: bfloat16 [16384, 1024], P(('ctx', 'head')), may hold values from -6 to 6
- attn_output: bfloat16 [16384, 8192], P(('ctx', 'head')), may hold values from -6 to 6
- grad_output: bfloat16 [16384, 8192], P(('ctx', 'head')), may hold values from -6 to 6
- doc_ids: int32 [16384], replicated, may hold values from 0 to 63, never falling along the last dimension, each value on 1 to 1024 neighbouring positions
Outputs:
- grad_queries: bfloat16 [16384, 8192], P(('ctx', 'head'))
- key_state_gradient: bfloat16 [16384, 1024], P(('ctx', 'head'))
- value_state_gradient: bfloat16 [16384, 1024], P(('ctx', 'head'))
All inputs are finite; a program needn't handle non-finite values.
Results may differ from a plain program's by a relative error of at most 0.005.
Values may be sent and summed in bfloat16 or wider, within the bound.
No kernel may reach another device: no remote copies, remote signals or barrier semaphores. Data moves between devices by JAX's collectives and lax.ppermute only.
A program may use at most 64 MiB of HBM per device.

v0:
```python
import math

import jax
import jax.numpy as jnp
from jax import lax
from jax.sharding import PartitionSpec as P

QUERY_HEAD_COUNT = 64
KEY_VALUE_HEADS = 8
HEAD_SIZE = 128


def from_behind(value, axis, steps):
    count = lax.axis_size(axis)
    initial, last = (max(0, -steps), min(count, count - steps))
    return lax.ppermute(value, axis, [(source, source + steps) for source in range(initial, last)])


def contract_rows(left, right):
    return lax.dot_general(
        left, right, (((0,), (0,)), ((), ())), preferred_element_type=jnp.float32
    )


def contract_cols(left, right):
    return lax.dot_general(
        left, right, (((1,), (1,)), ((), ())), preferred_element_type=jnp.float32
    )


def attend(
    query_block, grad_block, row_delta, keys, values, seg_query, seg_key, pos_query, pos_key
):
    score_scale = 1.0 / math.sqrt(HEAD_SIZE)
    group = query_block.shape[0]
    head_count = query_block.shape[1] // HEAD_SIZE
    block = min(512, group)
    grad_key = jnp.zeros((keys.shape[0], HEAD_SIZE), jnp.float32)
    grad_value = jnp.zeros((keys.shape[0], HEAD_SIZE), jnp.float32)
    head_columns = []
    for head_index in range(head_count):
        columns = slice(head_index * HEAD_SIZE, (head_index + 1) * HEAD_SIZE)
        row_parts = []
        for block_index in range(group // block):
            rows = slice(block_index * block, (block_index + 1) * block)
            query_part = query_block[rows, columns]
            grad_part = grad_block[rows, columns]
            visible = (seg_key[None, :] == seg_query[rows][:, None]) & (
                pos_key[None, :] <= pos_query[rows][:, None]
            )
            scores = contract_cols(query_part, keys) * score_scale
            masked = jnp.where(visible, scores, -1e30)
            largest = jnp.max(masked, axis=-1, keepdims=True)
            weights = jnp.where(visible, jnp.exp(masked - largest), 0.0)
            probs = weights / jnp.sum(weights, axis=-1, keepdims=True)
            probs_low = probs.astype(jnp.bfloat16)
            grad_value = grad_value + contract_rows(probs_low, grad_part)
            grad_probs = contract_cols(grad_part, values)
            grad_scores = (probs * (grad_probs - row_delta[rows, head_index][:, None])).astype(
                jnp.bfloat16
            )
            row_parts.append(
                jnp.dot(grad_scores, keys, preferred_element_type=jnp.float32) * score_scale
            )
            grad_key = grad_key + contract_rows(grad_scores, query_part) * score_scale
        head_columns.append(jnp.concatenate(row_parts, axis=0))
    return (jnp.concatenate(head_columns, axis=1), grad_key, grad_value)


def repeat_heads(hidden_states, replica_count):
    total_row_count = hidden_states.shape[0]
    expanded_heads = jnp.broadcast_to(
        hidden_states.reshape(total_row_count, KEY_VALUE_HEADS, 1, HEAD_SIZE),
        (total_row_count, KEY_VALUE_HEADS, replica_count, HEAD_SIZE),
    )
    return expanded_heads.reshape(total_row_count, KEY_VALUE_HEADS * replica_count * HEAD_SIZE)


def on_device(queries, key_state_rows, value_state_rows, attn_output, grad_output, doc_ids):
    head_placements = lax.axis_size("head")
    total_row_count = queries.shape[0]
    group = total_row_count * head_placements
    per_device = QUERY_HEAD_COUNT // head_placements
    replica_count = head_placements // KEY_VALUE_HEADS
    query_block, out_block, grad_block = (
        lax.all_to_all(queries, "head", split_axis=1, concat_axis=0, tiled=True),
        lax.all_to_all(attn_output, "head", split_axis=1, concat_axis=0, tiled=True),
        lax.all_to_all(grad_output, "head", split_axis=1, concat_axis=0, tiled=True),
    )
    row_delta = jnp.sum(
        (grad_block.astype(jnp.float32) * out_block.astype(jnp.float32)).reshape(
            group, per_device, HEAD_SIZE
        ),
        axis=-1,
    )
    key_local, value_local = (
        lax.all_to_all(
            repeat_heads(key_state_rows, replica_count),
            "head",
            split_axis=1,
            concat_axis=0,
            tiled=True,
        ),
        lax.all_to_all(
            repeat_heads(value_state_rows, replica_count),
            "head",
            split_axis=1,
            concat_axis=0,
            tiled=True,
        ),
    )
    key_prior, value_prior = from_behind((key_local, value_local), "ctx", 1)
    context = lax.axis_index("ctx")
    seg_query = lax.dynamic_slice_in_dim(doc_ids, context * group, group, 0)
    seg_prior = lax.dynamic_slice_in_dim(doc_ids, jnp.maximum(context - 1, 0) * group, group, 0)
    seg_prior = jnp.where(context > 0, seg_prior, -1)
    pos_query = jnp.arange(group, dtype=jnp.int32) + group
    pos_key = jnp.arange(2 * group, dtype=jnp.int32)
    keys_all = jnp.concatenate([key_prior, key_local], axis=0)
    values_all = jnp.concatenate([value_prior, value_local], axis=0)
    seg_all = jnp.concatenate([seg_prior, seg_query], axis=0)
    grad_query, grad_key, grad_value = attend(
        query_block,
        grad_block,
        row_delta,
        keys_all,
        values_all,
        seg_query,
        seg_all,
        pos_query,
        pos_key,
    )
    grad_query, key_before, key_here, value_before, value_here = (
        grad_query,
        grad_key[:group],
        grad_key[group:],
        grad_value[:group],
        grad_value[group:],
    )
    key_after, value_after = from_behind((key_before, value_before), "ctx", -1)
    grad_queries = lax.all_to_all(
        grad_query.astype(jnp.bfloat16), "head", split_axis=0, concat_axis=1, tiled=True
    )
    key_token_rows, value_token_rows = (
        lax.all_to_all(key_here + key_after, "head", split_axis=0, concat_axis=1, tiled=True),
        lax.all_to_all(value_here + value_after, "head", split_axis=0, concat_axis=1, tiled=True),
    )
    key_state_gradient = jnp.sum(
        key_token_rows.reshape(total_row_count, KEY_VALUE_HEADS, replica_count, HEAD_SIZE), axis=2
    ).reshape(total_row_count, KEY_VALUE_HEADS * HEAD_SIZE)
    value_state_gradient = jnp.sum(
        value_token_rows.reshape(total_row_count, KEY_VALUE_HEADS, replica_count, HEAD_SIZE), axis=2
    ).reshape(total_row_count, KEY_VALUE_HEADS * HEAD_SIZE)
    return (
        grad_queries,
        key_state_gradient.astype(jnp.bfloat16),
        value_state_gradient.astype(jnp.bfloat16),
    )


def solution(mesh):
    return jax.shard_map(
        on_device,
        mesh=mesh,
        in_specs=(
            P(("ctx", "head"), None),
            P(("ctx", "head"), None),
            P(("ctx", "head"), None),
            P(("ctx", "head"), None),
            P(("ctx", "head"), None),
            P(),
        ),
        out_specs=(P(("ctx", "head"), None), P(("ctx", "head"), None), P(("ctx", "head"), None)),
        check_vma=False,
    )
```

profile of v0, /device:TPU:417, one launch (start us, length us, event | category | flops | bytes accessed | tf_op | source)
XLA Modules:
  0.0 178.2 jit_solution(8607992369744974900)
XLA Ops:
  2.2 7.8 %all-to-all-start = ((bf16[32,32,128]{2,0,1:T(8,128)(2,1)}), bf16[32,32,128]{2,0,1:T(8,128)(2,1)S(1)}, u32[]{:S(2)}, u32[]{:S(2)}) async-start(bf16[32,32,128]{2,0,1:T(8,128)(2,1)} %bitcast), calls=%async_computation | async-start | bytes 524288 | tf_op jit(solution)/shard_map/all_to_all | solution.py:97
  10.9 8.0 %all-to-all-done = bf16[32,32,128]{2,0,1:T(8,128)(2,1)S(1)} async-done(((bf16[32,32,128]{2,0,1:T(8,128)(2,1)}), bf16[32,32,128]{2,0,1:T(8,128)(2,1)S(1)}, u32[]{:S(2)}, u32[]{:S(2)}) %all-to-all-start) | async-done | bytes 262176 | tf_op jit(solution)/shard_map/all_to_all | solution.py:97
  19.6 4.4 %all-to-all-start.2 = ((bf16[32,32,128]{2,0,1:T(8,128)(2,1)}), bf16[32,32,128]{2,0,1:T(8,128)(2,1)}, u32[]{:S(2)}, u32[]{:S(2)}) async-start(bf16[32,32,128]{2,0,1:T(8,128)(2,1)} %bitcast.6), calls=%async_computation.2 | async-start | bytes 524288 | tf_op jit(solution)/shard_map/all_to_all | solution.py:104
  24.1 1.9 %copy.49 = bf16[4,32,8,256]{3,2,0,1:T(8,128)(2,1)} copy(bf16[4,32,8,256]{3,2,1,0:T(8,128)(2,1)} %bitcast.180) | data formatting | bytes 1048576 | tf_op jit(solution)/shard_map/all_to_all | solution.py:88
  26.0 7.2 %all-to-all-done.2 = bf16[32,32,128]{2,0,1:T(8,128)(2,1)} async-done(((bf16[32,32,128]{2,0,1:T(8,128)(2,1)}), bf16[32,32,128]{2,0,1:T(8,128)(2,1)}, u32[]{:S(2)}, u32[]{:S(2)}) %all-to-all-start.2) | async-done | bytes 262176 | tf_op jit(solution)/shard_map/all_to_all | solution.py:104
  33.1 3.8 %all-to-all-start.3 = ((bf16[32,32,256]{2,0,1:T(8,128)(2,1)}), bf16[32,32,256]{2,0,1:T(8,128)(2,1)S(1)}, u32[]{:S(2)}, u32[]{:S(2)}) async-start(bf16[32,32,256]{2,0,1:T(8,128)(2,1)} %bitcast.150), calls=%async_computation.3 | async-start | bytes 1048576 | tf_op jit(solution)/shard_map/all_to_all | solution.py:88
  37.8 10.8 %all-to-all-done.3 = bf16[32,32,256]{2,0,1:T(8,128)(2,1)S(1)} async-done(((bf16[32,32,256]{2,0,1:T(8,128)(2,1)}), bf16[32,32,256]{2,0,1:T(8,128)(2,1)S(1)}, u32[]{:S(2)}, u32[]{:S(2)}) %all-to-all-start.3) | async-done | bytes 524320 | tf_op jit(solution)/shard_map/all_to_all | solution.py:88
  48.6 4.0 %all-to-all-start.4 = ((bf16[32,32,256]{2,0,1:T(8,128)(2,1)}), bf16[32,32,256]{2,0,1:T(8,128)(2,1)S(1)}, u32[]{:S(2)}, u32[]{:S(2)}) async-start(bf16[32,32,256]{2,0,1:T(8,128)(2,1)} %bitcast.149), calls=%async_computation.4 | async-start | bytes 1048576 | tf_op jit(solution)/shard_map/all_to_all | solution.py:87
  54.2 10.1 %all-to-all-done.4 = bf16[32,32,256]{2,0,1:T(8,128)(2,1)S(1)} async-done(((bf16[32,32,256]{2,0,1:T(8,128)(2,1)}), bf16[32,32,256]{2,0,1:T(8,128)(2,1)S(1)}, u32[]{:S(2)}, u32[]{:S(2)}) %all-to-all-start.4) | async-done | bytes 524320 | tf_op jit(solution)/shard_map/all_to_all | solution.py:87
  64.2 4.0 %all-to-all-start.1 = ((bf16[32,32,256]{2,0,1:T(8,128)(2,1)}), bf16[32,32,256]{2,0,1:T(8,128)(2,1)S(1)}, u32[]{:S(2)}, u32[]{:S(2)}) async-start(bf16[32,32,256]{2,0,1:T(8,128)(2,1)} %bitcast.151), calls=%async_computation.1 | async-start | bytes 1048576 | tf_op jit(solution)/shard_map/all_to_all | solution.py:86
  68.2 2.6 %collective-permute-start = (bf16[1024,128]{1,0:T(8,128)(2,1)S(1)}, bf16[1024,128]{1,0:T(8,128)(2,1)}, u32[]{:S(2)}, u32[]{:S(2)}) collective-permute-start(bf16[1024,128]{1,0:T(8,128)(2,1)S(1)} %bitcast.160), channel_id=1, source_target_pairs={{0,32},{32,64},{64,96},{96,128},{128,160},{160,192},{192,224},{224... | collective-permute-start | bytes 786440 | tf_op jit(solution)/shard_map/ppermute | solution.py:16
  70.9 2.8 %collective-permute-start.1 = (bf16[1024,128]{1,0:T(8,128)(2,1)}, bf16[1024,128]{1,0:T(8,128)(2,1)}, u32[]{:S(2)}, u32[]{:S(2)}) collective-permute-start(bf16[1024,128]{1,0:T(8,128)(2,1)} %bitcast.8), channel_id=1, source_target_pairs={{0,32},{32,64},{64,96},{96,128},{128,160},{160,192},{192,224},{224... | collective-permute-start | bytes 786440 | tf_op jit(solution)/shard_map/ppermute | solution.py:16
  76.1 3.8 %all-to-all-done.1 = bf16[32,32,256]{2,0,1:T(8,128)(2,1)S(1)} async-done(((bf16[32,32,256]{2,0,1:T(8,128)(2,1)}), bf16[32,32,256]{2,0,1:T(8,128)(2,1)S(1)}, u32[]{:S(2)}, u32[]{:S(2)}) %all-to-all-start.1) | async-done | bytes 524320 | tf_op jit(solution)/shard_map/all_to_all | solution.py:86
  83.2 2.9 %fusion.6 = (f32[512]{0:T(512)S(1)}, f32[512]{0:T(512)S(1)}, f32[2048,512]{1,0:T(8,128)S(1)}) fusion(s32[512]{0:T(512)S(1)} %get-tuple-element.25, s32[512]{0:T(512)S(1)} %get-tuple-element.20, s32[2048]{0:T(1024)S(1)} %pad_add_fusion, f32[2048,512]{1,0:T(8,128)S(1)} %fusion.41, s32[512]{0:T(512)S(1)} %get-tuple-element.26, s32[512]{0:T(512)S(1)} %get-tuple-element.19, ...), kind=kOutput, calls=%fused_computation.20 | convolution fusion | flops 282065920 | bytes 9064448 | tf_op jit(solution)/shard_map/dot_general | solution.py:26
  86.1 5.0 %fusion.12 = (f32[512]{0:T(512)S(1)}, f32[512]{0:T(512)S(1)}, f32[512]{0:T(512)S(1)}, f32[512]{0:T(512)S(1)}, f32[2048,512]{1,0:T(8,128)S(1)}) fusion(f32[2048,512]{1,0:T(8,128)S(1)} %get-tuple-element.23, f32[512]{0:T(512)S(1)} %get-tuple-element.13, s32[512]{0:T(512)S(1)} %get-tuple-element.25, s32[512]{0:T(512)S(1)} %get-tuple-element.20, ...), kind=kOutput, calls=%fused_computation.32 | convolution fusion | flops 292550656 | bytes 17461248 | tf_op jit(solution)/shard_map/dot_general | solution.py:26
  92.8 1.9 %convolution_add_fusion.2 = f32[2048,128]{1,0:T(8,128)S(1)} fusion(f32[2048,128]{1,0:T(8,128)S(1)} %fusion.22, bf16[1024,256]{1,0:T(8,128)(2,1)S(1)} %bitcast.171, f32[2048,512]{1,0:T(8,128)S(1)} %fusion.41, f32[512]{0:T(512)S(1)} %get-tuple-element.12, f32[512]{0:T(512)S(1)} %get-tuple-element.14, s32[512]{0:T(512)S(1)} %get-tuple-element.26, ...), kind=kOutput, calls=%fused_computation.26 | convolution fusion | flops 278134784 | bytes 6438912 | tf_op jit(solution)/shard_map/dot_general | solution.py:20
  94.8 3.2 %fusion.16 = (f32[512]{0:T(512)S(1)}, f32[512]{0:T(512)S(1)}) fusion(f32[2048,512]{1,0:T(8,128)S(1)} %get-tuple-element.24, f32[512]{0:T(512)S(1)} %get-tuple-element.8, s32[512]{0:T(512)S(1)} %get-tuple-element.25, s32[512]{0:T(512)S(1)} %get-tuple-element.20, s32[2048]{0:T(1024)S(1)} %pad_add_fusion, f32[512]{0:T(512)S(1)} %get-tuple-element.11, ...), kind=kLoop, calls=%fused_computation.36 | loop fusion | flops 16776192 | bytes 8413184 | tf_op jit(solution)/shard_map/reduce_sum | solution.py:55
  102.4 2.6 %collective-permute-start.3 = (f32[1024,128]{1,0:T(8,128)}, f32[1024,128]{1,0:T(8,128)S(1)}, u32[]{:S(2)}, u32[]{:S(2)}) collective-permute-start(f32[1024,128]{1,0:T(8,128)} %slice.99), channel_id=1, source_target_pairs={{32,0},{64,32},{96,64},{128,96},{160,128},{192,160},{224,192},{256... | collective-permute-start | bytes 1572872 | tf_op jit(solution)/shard_map/ppermute | solution.py:16
  105.0 2.8 %fusion.3 = bf16[512,2048]{0,1:T(8,128)(2,1)S(1)} fusion(f32[512]{0:T(512)S(1)} %get-tuple-element.3, bf16[1024,256]{1,0:T(8,128)(2,1)S(1)} %bitcast.174, bf16[1024,128]{1,0:T(8,128)(2,1)} %bitcast.8, bf16[1024,128]{1,0:T(8,128)(2,1)} %collective-permute-done.1, f32[512]{0:T(512)S(1)} %get-tuple-element.7, f32[512]{0:T(512)S(1)} %get-tuple-element.13, ...), kind=kOutput, calls=%fused_computation.10 | convolution fusion | flops 281018368 | bytes 6965248 | tf_op jit(solution)/shard_map/dot_general | solution.py:26
  108.5 2.8 %fusion.2 = bf16[512,2048]{0,1:T(8,128)(2,1)S(1)} fusion(f32[512]{0:T(512)S(1)} %get-tuple-element.6, bf16[1024,256]{1,0:T(8,128)(2,1)S(1)} %bitcast.175, bf16[1024,128]{1,0:T(8,128)(2,1)} %bitcast.8, bf16[1024,128]{1,0:T(8,128)(2,1)} %collective-permute-done.1, f32[512]{0:T(512)S(1)} %get-tuple-element.12, f32[512]{0:T(512)S(1)} %get-tuple-element.14, ...), kind=kOutput, calls=%fused_computation.7 | convolution fusion | flops 281018368 | bytes 6965248 | tf_op jit(solution)/shard_map/dot_general | solution.py:26
  115.6 2.8 %fusion.1 = bf16[512,2048]{0,1:T(8,128)(2,1)S(1)} fusion(f32[512]{0:T(512)S(1)} %get-tuple-element.5, bf16[1024,256]{1,0:T(8,128)(2,1)S(1)} %bitcast.176, bf16[1024,128]{1,0:T(8,128)(2,1)} %bitcast.8, bf16[1024,128]{1,0:T(8,128)(2,1)} %collective-permute-done.1, f32[512]{0:T(512)S(1)} %get-tuple-element.15, f32[512]{0:T(512)S(1)} %get-tuple-element.8, ...), kind=kOutput, calls=%fused_computation.4 | convolution fusion | flops 281018368 | bytes 6965248 | tf_op jit(solution)/shard_map/dot_general | solution.py:26
  118.4 3.2 %fusion = bf16[512,2048]{0,1:T(8,128)(2,1)S(1)} fusion(f32[512]{0:T(512)S(1)} %get-tuple-element.4, bf16[1024,256]{1,0:T(8,128)(2,1)S(1)} %bitcast.177, bf16[1024,128]{1,0:T(8,128)(2,1)} %bitcast.8, bf16[1024,128]{1,0:T(8,128)(2,1)} %collective-permute-done.1, f32[512]{0:T(512)S(1)} %get-tuple-element.16, f32[512]{0:T(512)S(1)} %get-tuple-element.11, ...), kind=kOutput, calls=%fused_computation.1 | convolution fusion | flops 281018368 | bytes 6965248 | tf_op jit(solution)/shard_map/dot_general | solution.py:26
  121.7 1.9 %fusion.26 = bf16[512,128]{1,0:T(8,128)(2,1)S(1)} fusion(bf16[512,2048]{0,1:T(8,128)(2,1)S(1)} %fusion.1, bf16[1024,128]{1,0:T(8,128)(2,1)S(1)} %bitcast.167, bf16[1024,128]{1,0:T(8,128)(2,1)} %collective-permute-done), kind=kOutput, calls=%fused_computation.50 | convolution fusion | flops 269615104 | bytes 2752512 | tf_op jit(solution)/shard_map/dot_general | solution.py:63
  126.2 8.5 %all-to-all-start.5 = ((bf16[32,32,256]{2,1,0:T(8,128)(2,1)}), bf16[32,32,256]{2,1,0:T(8,128)(2,1)S(1)}, u32[]{:S(2)}, u32[]{:S(2)}) async-start(bf16[32,32,256]{2,1,0:T(8,128)(2,1)} %pad_maximum_fusion.2), calls=%async_computation.5 | async-start | bytes 1048576 | tf_op jit(solution)/shard_map/all_to_all | solution.py:141
  134.7 2.4 %convolution_add_fusion.4 = f32[2048,128]{1,0:T(8,128)S(1)} fusion(f32[2048,128]{1,0:T(8,128)S(1)} %convolution_add_fusion.5, bf16[512,2048]{0,1:T(8,128)(2,1)} %copy-done.1, bf16[1024,256]{1,0:T(8,128)(2,1)S(1)} %bitcast.158), kind=kOutput, calls=%fused_computation.29 | convolution fusion | flops 268697600 | bytes 4325376 | tf_op jit(solution)/shard_map/dot_general | solution.py:20
  138.7 2.6 %collective-permute-start.2 = (f32[1024,128]{1,0:T(8,128)}, f32[1024,128]{1,0:T(8,128)S(1)}, u32[]{:S(2)}, u32[]{:S(2)}) collective-permute-start(f32[1024,128]{1,0:T(8,128)} %slice.97), channel_id=1, source_target_pairs={{32,0},{64,32},{96,64},{128,96},{160,128},{192,160},{224,192},{256... | collective-permute-start | bytes 1572872 | tf_op jit(solution)/shard_map/ppermute | solution.py:16
  142.2 4.0 %all-to-all-done.5 = bf16[32,32,256]{2,1,0:T(8,128)(2,1)S(1)} async-done(((bf16[32,32,256]{2,1,0:T(8,128)(2,1)}), bf16[32,32,256]{2,1,0:T(8,128)(2,1)S(1)}, u32[]{:S(2)}, u32[]{:S(2)}) %all-to-all-start.5) | async-done | bytes 524320 | tf_op jit(solution)/shard_map/all_to_all | solution.py:141
  146.2 4.0 %all-to-all-start.7 = ((f32[32,32,128]{2,1,0:T(8,128)}), f32[32,32,128]{2,1,0:T(8,128)S(1)}, u32[]{:S(2)}, u32[]{:S(2)}) async-start(f32[32,32,128]{2,1,0:T(8,128)} %bitcast.27), calls=%async_computation.7 | async-start | bytes 1048576 | tf_op jit(solution)/shard_map/all_to_all | solution.py:146
  150.2 3.6 %collective-permute-done.2 = f32[1024,128]{1,0:T(8,128)S(1)} collective-permute-done((f32[1024,128]{1,0:T(8,128)}, f32[1024,128]{1,0:T(8,128)S(1)}, u32[]{:S(2)}, u32[]{:S(2)}) %collective-permute-start.2) | collective-permute-done | bytes 524320 | tf_op jit(solution)/shard_map/ppermute | solution.py:16
  154.6 7.3 %all-to-all-done.7 = f32[32,32,128]{2,1,0:T(8,128)S(1)} async-done(((f32[32,32,128]{2,1,0:T(8,128)}), f32[32,32,128]{2,1,0:T(8,128)S(1)}, u32[]{:S(2)}, u32[]{:S(2)}) %all-to-all-start.7) | async-done | bytes 524320 | tf_op jit(solution)/shard_map/all_to_all | solution.py:146
  161.9 4.0 %all-to-all-start.6 = ((f32[32,32,128]{2,1,0:T(8,128)}), f32[32,32,128]{2,1,0:T(8,128)S(1)}, u32[]{:S(2)}, u32[]{:S(2)}) async-start(f32[32,32,128]{2,1,0:T(8,128)} %bitcast.24), calls=%async_computation.6 | async-start | bytes 1048576 | tf_op jit(solution)/shard_map/all_to_all | solution.py:145
  167.4 10.2 %all-to-all-done.6 = f32[32,32,128]{2,1,0:T(8,128)S(1)} async-done(((f32[32,32,128]{2,1,0:T(8,128)}), f32[32,32,128]{2,1,0:T(8,128)S(1)}, u32[]{:S(2)}, u32[]{:S(2)}) %all-to-all-start.6) | async-done | bytes 524320 | tf_op jit(solution)/shard_map/all_to_all | solution.py:145
  (56 shorter events, 30.2 us)
Async XLA Ops:
  0.6 0.8 copy-start
  0.6 36.3 %copy-start.6 = (bf16[32,8192]{1,0:T(8,128)(2,1)S(1)}, bf16[32,8192]{1,0:T(8,128)(2,1)}, u32[]{:S(2)}) copy-start(bf16[32,8192]{1,0:T(8,128)(2,1)} %param.9) | copy-start | bytes 1572868
  0.7 51.9 %copy-start.7 = (bf16[32,8192]{1,0:T(8,128)(2,1)S(1)}, bf16[32,8192]{1,0:T(8,128)(2,1)}, u32[]{:S(2)}) copy-start(bf16[32,8192]{1,0:T(8,128)(2,1)} %param.6) | copy-start | bytes 1572868
  2.2 16.7 %all-to-all-start = ((bf16[32,32,128]{2,0,1:T(8,128)(2,1)}), bf16[32,32,128]{2,0,1:T(8,128)(2,1)S(1)}, u32[]{:S(2)}, u32[]{:S(2)}) async-start(bf16[32,32,128]{2,0,1:T(8,128)(2,1)} %bitcast), calls=%async_computation | async-start | bytes 524288 | tf_op jit(solution)/shard_map/all_to_all | solution.py:97
  19.6 13.5 %all-to-all-start.2 = ((bf16[32,32,128]{2,0,1:T(8,128)(2,1)}), bf16[32,32,128]{2,0,1:T(8,128)(2,1)}, u32[]{:S(2)}, u32[]{:S(2)}) async-start(bf16[32,32,128]{2,0,1:T(8,128)(2,1)} %bitcast.6), calls=%async_computation.2 | async-start | bytes 524288 | tf_op jit(solution)/shard_map/all_to_all | solution.py:104
  33.1 15.4 %all-to-all-start.3 = ((bf16[32,32,256]{2,0,1:T(8,128)(2,1)}), bf16[32,32,256]{2,0,1:T(8,128)(2,1)S(1)}, u32[]{:S(2)}, u32[]{:S(2)}) async-start(bf16[32,32,256]{2,0,1:T(8,128)(2,1)} %bitcast.150), calls=%async_computation.3 | async-start | bytes 1048576 | tf_op jit(solution)/shard_map/all_to_all | solution.py:88
  48.6 15.7 %all-to-all-start.4 = ((bf16[32,32,256]{2,0,1:T(8,128)(2,1)}), bf16[32,32,256]{2,0,1:T(8,128)(2,1)S(1)}, u32[]{:S(2)}, u32[]{:S(2)}) async-start(bf16[32,32,256]{2,0,1:T(8,128)(2,1)} %bitcast.149), calls=%async_computation.4 | async-start | bytes 1048576 | tf_op jit(solution)/shard_map/all_to_all | solution.py:87
  64.2 15.7 %all-to-all-start.1 = ((bf16[32,32,256]{2,0,1:T(8,128)(2,1)}), bf16[32,32,256]{2,0,1:T(8,128)(2,1)S(1)}, u32[]{:S(2)}, u32[]{:S(2)}) async-start(bf16[32,32,256]{2,0,1:T(8,128)(2,1)} %bitcast.151), calls=%async_computation.1 | async-start | bytes 1048576 | tf_op jit(solution)/shard_map/all_to_all | solution.py:86
  68.2 11.7 %collective-permute-start = (bf16[1024,128]{1,0:T(8,128)(2,1)S(1)}, bf16[1024,128]{1,0:T(8,128)(2,1)}, u32[]{:S(2)}, u32[]{:S(2)}) collective-permute-start(bf16[1024,128]{1,0:T(8,128)(2,1)S(1)} %bitcast.160), channel_id=1, source_target_pairs={{0,32},{32,64},{64,96},{96,128},{128,160},{160,192},{192,224},{224... | collective-permute-start | bytes 786440 | tf_op jit(solution)/shard_map/ppermute | solution.py:16
  70.9 34.1 %collective-permute-start.1 = (bf16[1024,128]{1,0:T(8,128)(2,1)}, bf16[1024,128]{1,0:T(8,128)(2,1)}, u32[]{:S(2)}, u32[]{:S(2)}) collective-permute-start(bf16[1024,128]{1,0:T(8,128)(2,1)} %bitcast.8), channel_id=1, source_target_pairs={{0,32},{32,64},{64,96},{96,128},{128,160},{160,192},{192,224},{224... | collective-permute-start | bytes 786440 | tf_op jit(solution)/shard_map/ppermute | solution.py:16
  101.5 6.4 %copy-start.4 = (f32[2048,128]{1,0:T(8,128)}, f32[2048,128]{1,0:T(8,128)S(1)}, u32[]{:S(2)}) copy-start(f32[2048,128]{1,0:T(8,128)S(1)} %convolution_add_fusion) | copy-start | bytes 3145732
  102.4 39.0 %collective-permute-start.3 = (f32[1024,128]{1,0:T(8,128)}, f32[1024,128]{1,0:T(8,128)S(1)}, u32[]{:S(2)}, u32[]{:S(2)}) collective-permute-start(f32[1024,128]{1,0:T(8,128)} %slice.99), channel_id=1, source_target_pairs={{32,0},{64,32},{96,64},{128,96},{160,128},{192,160},{224,192},{256... | collective-permute-start | bytes 1572872 | tf_op jit(solution)/shard_map/ppermute | solution.py:16
  118.4 3.2 %copy-start.1 = (bf16[512,2048]{0,1:T(8,128)(2,1)}, bf16[512,2048]{0,1:T(8,128)(2,1)S(1)}, u32[]{:S(2)}) copy-start(bf16[512,2048]{0,1:T(8,128)(2,1)S(1)} %fusion.1) | copy-start | bytes 6291460
  121.7 3.6 %copy-start.2 = (bf16[512,2048]{0,1:T(8,128)(2,1)}, bf16[512,2048]{0,1:T(8,128)(2,1)S(1)}, u32[]{:S(2)}) copy-start(bf16[512,2048]{0,1:T(8,128)(2,1)S(1)} %fusion) | copy-start | bytes 6291460
  126.2 20.0 %all-to-all-start.5 = ((bf16[32,32,256]{2,1,0:T(8,128)(2,1)}), bf16[32,32,256]{2,1,0:T(8,128)(2,1)S(1)}, u32[]{:S(2)}, u32[]{:S(2)}) async-start(bf16[32,32,256]{2,1,0:T(8,128)(2,1)} %pad_maximum_fusion.2), calls=%async_computation.5 | async-start | bytes 1048576 | tf_op jit(solution)/shard_map/all_to_all | solution.py:141
  134.7 2.5 %copy-start.3 = (bf16[512,2048]{0,1:T(8,128)(2,1)S(1)}, bf16[512,2048]{0,1:T(8,128)(2,1)}, u32[]{:S(2)}) copy-start(bf16[512,2048]{0,1:T(8,128)(2,1)} %copy-done.2) | copy-start | bytes 6291460
  134.7 6.6 %copy-start.5 = (f32[2048,128]{1,0:T(8,128)S(1)}, f32[2048,128]{1,0:T(8,128)}, u32[]{:S(2)}) copy-start(f32[2048,128]{1,0:T(8,128)} %copy-done.4) | copy-start | bytes 3145732
  138.7 15.1 %collective-permute-start.2 = (f32[1024,128]{1,0:T(8,128)}, f32[1024,128]{1,0:T(8,128)S(1)}, u32[]{:S(2)}, u32[]{:S(2)}) collective-permute-start(f32[1024,128]{1,0:T(8,128)} %slice.97), channel_id=1, source_target_pairs={{32,0},{64,32},{96,64},{128,96},{160,128},{192,160},{224,192},{256... | collective-permute-start | bytes 1572872 | tf_op jit(solution)/shard_map/ppermute | solution.py:16
  146.2 15.7 %all-to-all-start.7 = ((f32[32,32,128]{2,1,0:T(8,128)}), f32[32,32,128]{2,1,0:T(8,128)S(1)}, u32[]{:S(2)}, u32[]{:S(2)}) async-start(f32[32,32,128]{2,1,0:T(8,128)} %bitcast.27), calls=%async_computation.7 | async-start | bytes 1048576 | tf_op jit(solution)/shard_map/all_to_all | solution.py:146
  161.9 15.7 %all-to-all-start.6 = ((f32[32,32,128]{2,1,0:T(8,128)}), f32[32,32,128]{2,1,0:T(8,128)S(1)}, u32[]{:S(2)}, u32[]{:S(2)}) async-start(f32[32,32,128]{2,1,0:T(8,128)} %bitcast.24), calls=%async_computation.6 | async-start | bytes 1048576 | tf_op jit(solution)/shard_map/all_to_all | solution.py:145
where the time goes:
time: 180 us; the launch traced here: 178 us
  waiting for transfers between devices  64.8 us (36%)
  starting transfers between devices  51.1 us (28%)
  matrix products  41.6 us (23%)
  local copies, waits for them, and re-layouts  11.7 us (6%)
  other arithmetic  7.97 us (4%)
    dot_general x8, matrix products, contract_cols(): lax.dot_general(left, right, (((1,), (1,)), ((), ())), preferred_element_...  22.9 us
    dot_general x8, matrix products, contract_rows(): lax.dot_general(left, right, (((0,), (0,)), ((), ())), preferred_element_...  11.6 us
    all_to_all x1, waiting for transfers between devices, on_device(): lax.all_to_all(grad_output, 'head', split_axis=1, concat_axis=0, tiled=True)  10.8 us
    ppermute x4, starting transfers between devices, from_behind(): lax.ppermute(value, axis, [(source, source + steps) for source in range(i...  10.7 us
    all_to_all x1, waiting for transfers between devices, on_device(): lax.all_to_all(key_here + key_after, 'head', split_axis=0, concat_axis=1,...  10.2 us
    all_to_all x1, waiting for transfers between devices, on_device(): lax.all_to_all(attn_output, 'head', split_axis=1, concat_axis=0, tiled=True)  10.1 us
    all_to_all x1, starting transfers between devices, on_device(): lax.all_to_all(grad_query.astype(jnp.bfloat16), 'head', split_axis=0, con...  8.49 us
    all_to_all x1, waiting for transfers between devices, on_device(): lax.all_to_all(repeat_heads(key_state_rows, replica_count), 'head', split...  8.04 us
  transfers between devices with their start and end apart: 12, of which 9 were waited for; matrix products, arithmetic and copies ran while one was open for 33% of the time, Pallas kernels for 0%

commit v1 on v0

v1 whole, which is shorter than its diff:
```python
import math

import jax
import jax.numpy as jnp
from jax import lax
from jax.experimental import pallas as pl
from jax.experimental.pallas import tpu as pltpu
from jax.sharding import PartitionSpec as P

QUERY_HEAD_COUNT = 64
KEY_VALUE_HEADS = 8
HEAD_SIZE = 128
HEADS_EACH = QUERY_HEAD_COUNT // KEY_VALUE_HEADS
COLUMNS = HEADS_EACH * HEAD_SIZE
BEHIND = 4
SCALE = 1.0 / math.sqrt(HEAD_SIZE)
LOG2E = math.log2(math.e)
VMEM = pl.BlockSpec(memory_space=pltpu.VMEM)


def params(megabytes):
    return pltpu.CompilerParams(vmem_limit_bytes=megabytes * 1024 * 1024)


def contract_last(left, right):
    return lax.dot_general(
        left, right, (((1,), (1,)), ((), ())), preferred_element_type=jnp.float32
    )


def pack_keys_kernel(key_ref, value_ref, out_ref):
    for c in range(KEY_VALUE_HEADS):
        columns = slice(c * HEAD_SIZE, (c + 1) * HEAD_SIZE)
        out_ref[c, :, :HEAD_SIZE] = key_ref[:, columns]
        out_ref[c, :, HEAD_SIZE:] = value_ref[:, columns]


def pack_keys(keys, values):
    rows = keys.shape[0]
    return pl.pallas_call(
        pack_keys_kernel,
        out_shape=jax.ShapeDtypeStruct((KEY_VALUE_HEADS, rows, 2 * HEAD_SIZE), jnp.bfloat16),
        in_specs=[VMEM] * 2,
        out_specs=VMEM,
        name="pack_keys",
    )(keys, values)


def pack_queries_kernel(query_ref, out_ref, grad_ref, packed_ref):
    rows = query_ref.shape[0]
    lane = lax.broadcasted_iota(jnp.int32, (rows, HEAD_SIZE), 1)
    for c in range(KEY_VALUE_HEADS):
        columns = slice(c * COLUMNS, (c + 1) * COLUMNS)
        packed_ref[c, :, :COLUMNS] = query_ref[:, columns]
        packed_ref[c, :, COLUMNS : 2 * COLUMNS] = grad_ref[:, columns]
        terms = jnp.zeros((rows, HEAD_SIZE), jnp.float32)
        for h in range(HEADS_EACH):
            head = slice(c * COLUMNS + h * HEAD_SIZE, c * COLUMNS + (h + 1) * HEAD_SIZE)
            delta = jnp.sum(
                grad_ref[:, head].astype(jnp.float32) * out_ref[:, head].astype(jnp.float32),
                axis=-1,
                keepdims=True,
            )
            high = delta.astype(jnp.bfloat16).astype(jnp.float32)
            rest = delta - high
            middle = rest.astype(jnp.bfloat16).astype(jnp.float32)
            terms = jnp.where(lane == h, high, terms)
            terms = jnp.where(lane == HEADS_EACH + h, middle, terms)
            terms = jnp.where(lane == 2 * HEADS_EACH + h, rest - middle, terms)
        packed_ref[c, :, 2 * COLUMNS :] = terms.astype(jnp.bfloat16)


def pack_queries(queries, outputs, grads):
    rows = queries.shape[0]
    return pl.pallas_call(
        pack_queries_kernel,
        out_shape=jax.ShapeDtypeStruct(
            (KEY_VALUE_HEADS, rows, 2 * COLUMNS + HEAD_SIZE), jnp.bfloat16
        ),
        in_specs=[VMEM] * 3,
        out_specs=VMEM,
        name="pack_queries",
    )(queries, outputs, grads)


def attend_kernel(
    packed_ref, kv0, kv1, kv2, kv3, kv4, first_ref,
    grad_query_ref, out0, out1, out2, out3, out4,
    bias, key_turned, scores, delta, key_total, value_total,
):
    kv = (kv0, kv1, kv2, kv3, kv4)
    outs = (out0, out1, out2, out3, out4)
    block = kv0.shape[0]
    parts = len(kv)
    rows = [slice(j * block, (j + 1) * block) for j in range(parts)]
    first = first_ref[...]
    last = lax.broadcasted_iota(jnp.int32, (1, block), 1) + (parts - 1) * block
    for j in range(parts):
        key_at = lax.broadcasted_iota(jnp.int32, (block, block), 0) + j * block
        seen = (key_at >= first) & (key_at <= last)
        bias[rows[j], :] = jnp.where(seen, 0.0, -1e30)
        key_turned[:, rows[j]] = kv[j][:, :HEAD_SIZE].astype(jnp.float32).T.astype(jnp.bfloat16)
    terms = packed_ref[:, 2 * COLUMNS :].astype(jnp.float32).T
    delta[...] = (
        terms[:HEADS_EACH] + terms[HEADS_EACH : 2 * HEADS_EACH]
        + terms[2 * HEADS_EACH : 3 * HEADS_EACH]
    )
    key_total[...] = jnp.zeros_like(key_total)
    value_total[...] = jnp.zeros_like(value_total)

    def one_head(h, carry):
        at = pl.multiple_of(h * HEAD_SIZE, HEAD_SIZE)
        query = packed_ref[:, pl.ds(at, HEAD_SIZE)]
        grad = packed_ref[:, pl.ds(COLUMNS + at, HEAD_SIZE)]
        row_delta = delta[pl.ds(h, 1), :]
        largest = jnp.full((1, block), -jnp.inf, jnp.float32)
        for j in range(parts):
            part = contract_last(kv[j][:, :HEAD_SIZE], query) * (SCALE * LOG2E) + bias[rows[j], :]
            scores[rows[j], :] = part
            largest = jnp.maximum(largest, jnp.max(part, axis=0, keepdims=True))
        total = jnp.zeros((1, block), jnp.float32)
        for j in range(parts):
            part = jnp.exp2(scores[rows[j], :] - largest)
            scores[rows[j], :] = part
            total = total + jnp.sum(part, axis=0, keepdims=True)
        inverse = 1.0 / total
        query_grad = jnp.zeros((HEAD_SIZE, block), jnp.float32)
        for j in range(parts):
            probs = scores[rows[j], :] * inverse
            value_total[rows[j], :] += jnp.dot(
                probs.astype(jnp.bfloat16), grad, preferred_element_type=jnp.float32
            )
            grad_probs = contract_last(kv[j][:, HEAD_SIZE:], grad)
            grad_scores = (probs * (grad_probs - row_delta)).astype(jnp.bfloat16)
            key_total[rows[j], :] += jnp.dot(
                grad_scores, query, preferred_element_type=jnp.float32
            )
            query_grad = query_grad + jnp.dot(
                key_turned[:, rows[j]], grad_scores, preferred_element_type=jnp.float32
            )
        grad_query_ref[:, pl.ds(at, HEAD_SIZE)] = (query_grad * SCALE).T.astype(jnp.bfloat16)
        return carry

    lax.fori_loop(0, HEADS_EACH, one_head, 0)
    for j in range(parts):
        outs[j][:, :HEAD_SIZE] = (key_total[rows[j], :] * SCALE).astype(outs[j].dtype)
        outs[j][:, HEAD_SIZE:] = value_total[rows[j], :].astype(outs[j].dtype)


def attend(packed, kv, first):
    block = packed.shape[0]
    keys = block * len(kv)
    part = (block, 2 * HEAD_SIZE)
    return pl.pallas_call(
        attend_kernel,
        out_shape=[jax.ShapeDtypeStruct((block, COLUMNS), jnp.bfloat16)]
        + [jax.ShapeDtypeStruct(part, jnp.bfloat16)] * BEHIND
        + [jax.ShapeDtypeStruct(part, jnp.float32)],
        in_specs=[VMEM] * (2 + len(kv)),
        out_specs=[VMEM] * (1 + len(kv)),
        scratch_shapes=[
            pltpu.VMEM((keys, block), jnp.float32),
            pltpu.VMEM((HEAD_SIZE, keys), jnp.bfloat16),
            pltpu.VMEM((keys, block), jnp.float32),
            pltpu.VMEM((HEADS_EACH, block), jnp.float32),
            pltpu.VMEM((keys, HEAD_SIZE), jnp.float32),
            pltpu.VMEM((keys, HEAD_SIZE), jnp.float32),
        ],
        compiler_params=params(32),
        name="attend",
    )(packed, *kv, first)


def add_kernel(own_ref, ref1, ref2, ref3, ref4, out_ref):
    total = own_ref[...]
    for ref in (ref1, ref2, ref3, ref4):
        total = total + ref[...].astype(jnp.float32)
    out_ref[...] = total.astype(jnp.bfloat16)


def add_parts(own, others):
    return pl.pallas_call(
        add_kernel,
        out_shape=jax.ShapeDtypeStruct(own.shape, jnp.bfloat16),
        in_specs=[VMEM] * (1 + len(others)),
        out_specs=VMEM,
        name="add_parts",
    )(own, *others)


def unpack_queries_kernel(in_ref, out_ref):
    for c in range(KEY_VALUE_HEADS):
        out_ref[:, c * COLUMNS : (c + 1) * COLUMNS] = in_ref[c]


def unpack_queries(packed):
    rows = packed.shape[1]
    return pl.pallas_call(
        unpack_queries_kernel,
        out_shape=jax.ShapeDtypeStruct((rows, KEY_VALUE_HEADS * COLUMNS), jnp.bfloat16),
        in_specs=[VMEM],
        out_specs=VMEM,
        name="unpack_queries",
    )(packed)


def unpack_keys_kernel(in_ref, key_ref, value_ref):
    for c in range(KEY_VALUE_HEADS):
        columns = slice(c * HEAD_SIZE, (c + 1) * HEAD_SIZE)
        key_ref[:, columns] = in_ref[c, :, :HEAD_SIZE]
        value_ref[:, columns] = in_ref[c, :, HEAD_SIZE:]


def unpack_keys(packed):
    rows = packed.shape[1]
    shape = jax.ShapeDtypeStruct((rows, KEY_VALUE_HEADS * HEAD_SIZE), jnp.bfloat16)
    return pl.pallas_call(
        unpack_keys_kernel,
        out_shape=[shape, shape],
        in_specs=[VMEM],
        out_specs=[VMEM] * 2,
        name="unpack_keys",
    )(packed)


def on_device(queries, key_state_rows, value_state_rows, attn_output, grad_output, doc_ids):
    placements = lax.axis_size("head")
    contexts = lax.axis_size("ctx")
    rows = queries.shape[0]
    sharers = KEY_VALUE_HEADS
    blocks_each = placements // sharers
    block = rows * sharers
    teams = [[t * sharers + i for i in range(sharers)] for t in range(blocks_each)]

    def exchange(value):
        return lax.all_to_all(
            value, "head", split_axis=0, concat_axis=0, axis_index_groups=teams, tiled=True
        )

    def shift(value, steps):
        count = contexts * blocks_each
        pairs = [
            (source * sharers + i, (source + steps) * sharers + i)
            for source in range(count)
            if 0 <= source + steps < count
            for i in range(sharers)
        ]
        return lax.ppermute(value, ("ctx", "head"), pairs)

    at = lax.axis_index("ctx") * blocks_each + lax.axis_index("head") // sharers
    padded = jnp.concatenate([jnp.full((BEHIND * block,), -1, jnp.int32), doc_ids])
    seg_key = lax.dynamic_slice_in_dim(padded, at * block, (BEHIND + 1) * block, 0)
    seg_query = seg_key[BEHIND * block :]
    first = jnp.sum((seg_key[:, None] < seg_query[None, :]).astype(jnp.int32), axis=0)[None, :]

    own = exchange(pack_keys(key_state_rows, value_state_rows)).reshape(block, 2 * HEAD_SIZE)
    packed = exchange(pack_queries(queries, attn_output, grad_output))
    packed = packed.reshape(block, 2 * COLUMNS + HEAD_SIZE)
    kv = [shift(own, steps) for steps in range(BEHIND, 0, -1)] + [own]
    grad_query, *grad_kv = attend(packed, kv, first)
    grad_rows = exchange(grad_query.reshape(sharers, rows, COLUMNS))
    others = [shift(grad_kv[j], j - BEHIND) for j in range(BEHIND)]
    grad_own = add_parts(grad_kv[BEHIND], others)
    kv_rows = exchange(grad_own.reshape(sharers, rows, 2 * HEAD_SIZE))
    key_state_gradient, value_state_gradient = unpack_keys(kv_rows)
    return unpack_queries(grad_rows), key_state_gradient, value_state_gradient


def solution(mesh):
    split = P(("ctx", "head"), None)
    return jax.shard_map(
        on_device,
        mesh=mesh,
        in_specs=(split, split, split, split, split, P()),
        out_specs=(split, split, split),
        check_vma=False,
    )
```

time: 180 us -> 101 us (0.56)
  the two profiles are of different devices: /device:TPU:417 before, /device:TPU:248 now
where the time goes in v1:
time: 101 us; the launch traced here: 99.8 us
  starting transfers between devices  37 us (37%)
  Pallas kernels  24.8 us (25%)
  waiting for transfers between devices  23.8 us (24%)
  blocking collectives  10.8 us (11%)
  local copies, waits for them, and re-layouts  2.31 us (2%)
    ppermute x8, starting transfers between devices, shift(): return lax.ppermute(value, ('ctx', 'head'), pairs)  25.7 us
    pallas_call x1, Pallas kernels, attend(): pl.pallas_call(attend_kernel, out_shape=[jax.ShapeDtypeStruct((block, COL...  15.1 us
    all_to_all x3, waiting for transfers between devices, exchange(): lax.all_to_all(value, 'head', split_axis=0, concat_axis=0, axis_index_gro...  12 us
    ppermute x8, waiting for transfers between devices, shift(): return lax.ppermute(value, ('ctx', 'head'), pairs)  11.8 us
    all_to_all x3, starting transfers between devices, exchange(): lax.all_to_all(value, 'head', split_axis=0, concat_axis=0, axis_index_gro...  11.4 us
    all_to_all x1, blocking collectives, exchange(): lax.all_to_all(value, 'head', split_axis=0, concat_axis=0, axis_index_gro...  10.8 us
    pallas_call x1, Pallas kernels, pack_queries(): pl.pallas_call(pack_queries_kernel, out_shape=jax.ShapeDtypeStruct((KEY_V...  2.82 us
    unnamed x14, local copies, waits for them, and re-layouts  2.14 us
  transfers between devices with their start and end apart: 11, of which 8 were waited for; matrix products, arithmetic and copies ran while one was open for 0% of the time, Pallas kernels for 4%

profile of v1, /device:TPU:248, one launch (start us, length us, event | category | flops | bytes accessed | tf_op | source)
XLA Modules:
  0.0 99.8 jit_solution(9058129505456226440)
XLA Ops:
  0.6 1.6 %pack_keys.1 = bf16[8,32,256]{2,1,0:T(8,128)(2,1)} custom-call(bf16[32,1024]{1,0:T(8,128)(2,1)} %key_ref.1, bf16[32,1024]{1,0:T(8,128)(2,1)} %value_ref.1), custom_call_target="tpu_custom_call" | custom-call | tf_op jit(solution)/shard_map/pack_keys/pallas_call | solution.py:40
  2.2 4.3 %all-to-all-start.1 = ((bf16[8,32,256]{2,1,0:T(8,128)(2,1)}), bf16[8,32,256]{2,1,0:T(8,128)(2,1)S(1)}, u32[]{:S(2)}, u32[]{:S(2)}) async-start(bf16[8,32,256]{2,1,0:T(8,128)(2,1)} %pack_keys.1), calls=%async_computation.1 | async-start | bytes 262144 | tf_op jit(solution)/shard_map/all_to_all | solution.py:236
  6.5 2.8 %pack_queries.1 = bf16[8,32,2176]{2,1,0:T(8,128)(2,1)} custom-call(bf16[32,8192]{1,0:T(8,128)(2,1)} %query_ref.1, bf16[32,8192]{1,0:T(8,128)(2,1)} %out_ref.1, bf16[32,8192]{1,0:T(8,128)(2,1)} %grad_ref.1), custom_call_target="tpu_custom_call" | custom-call | tf_op jit(solution)/shard_map/pack_queries/pallas_call | solution.py:75
  9.3 3.3 %all-to-all-done.1 = bf16[8,32,256]{2,1,0:T(8,128)(2,1)S(1)} async-done(((bf16[8,32,256]{2,1,0:T(8,128)(2,1)}), bf16[8,32,256]{2,1,0:T(8,128)(2,1)S(1)}, u32[]{:S(2)}, u32[]{:S(2)}) %all-to-all-start.1) | async-done | bytes 131104 | tf_op jit(solution)/shard_map/all_to_all | solution.py:236
  12.6 3.6 %all-to-all-start = ((bf16[8,32,2176]{2,1,0:T(8,128)(2,1)}), bf16[8,32,2176]{2,1,0:T(8,128)(2,1)S(1)}, u32[]{:S(2)}, u32[]{:S(2)}) async-start(bf16[8,32,2176]{2,1,0:T(8,128)(2,1)} %pack_queries.1), calls=%async_computation | async-start | bytes 2228224 | tf_op jit(solution)/shard_map/all_to_all | solution.py:236
  16.2 0.1 pad_dynamic-slice_fusion.1
  16.3 4.7 %collective-permute-start.3 = (bf16[256,256]{1,0:T(8,128)(2,1)S(1)}, bf16[256,256]{1,0:T(8,128)(2,1)S(1)}, u32[]{:S(2)}, u32[]{:S(2)}) collective-permute-start(bf16[256,256]{1,0:T(8,128)(2,1)S(1)} %bitcast.6), channel_id=1, source_target_pairs={{0,8},{1,9},{2,10},{3,11},{4,12},{5,13},{6,14},{7,15},{8,16},{9,17... | collective-permute-start | bytes 393224 | tf_op jit(solution)/shard_map/ppermute | solution.py:248
  21.0 4.5 %collective-permute-start.2 = (bf16[256,256]{1,0:T(8,128)(2,1)S(1)}, bf16[256,256]{1,0:T(8,128)(2,1)S(1)}, u32[]{:S(2)}, u32[]{:S(2)}) collective-permute-start(bf16[256,256]{1,0:T(8,128)(2,1)S(1)} %bitcast.7), channel_id=1, source_target_pairs={{0,16},{1,17},{2,18},{3,19},{4,20},{5,21},{6,22},{7,23},{8,24},{9,... | collective-permute-start | bytes 393224 | tf_op jit(solution)/shard_map/ppermute | solution.py:248
  25.5 2.2 %collective-permute-start.1 = (bf16[256,256]{1,0:T(8,128)(2,1)S(1)}, bf16[256,256]{1,0:T(8,128)(2,1)S(1)}, u32[]{:S(2)}, u32[]{:S(2)}) collective-permute-start(bf16[256,256]{1,0:T(8,128)(2,1)S(1)} %bitcast.8), channel_id=1, source_target_pairs={{0,24},{1,25},{2,26},{3,27},{4,28},{5,29},{6,30},{7,31},{8,32},{9,... | collective-permute-start | bytes 393224 | tf_op jit(solution)/shard_map/ppermute | solution.py:248
  27.7 2.9 %collective-permute-start = (bf16[256,256]{1,0:T(8,128)(2,1)S(1)}, bf16[256,256]{1,0:T(8,128)(2,1)S(1)}, u32[]{:S(2)}, u32[]{:S(2)}) collective-permute-start(bf16[256,256]{1,0:T(8,128)(2,1)S(1)} %bitcast.9), channel_id=1, source_target_pairs={{0,32},{1,33},{2,34},{3,35},{4,36},{5,37},{6,38},{7,39},{8,40},{9,... | collective-permute-start | bytes 393224 | tf_op jit(solution)/shard_map/ppermute | solution.py:248
  30.7 0.1 pad_dynamic-slice_fusion
  30.7 0.2 convert_reduce_fusion
  31.0 1.8 %collective-permute-done.2.kv2 = bf16[256,256]{1,0:T(8,128)(2,1)S(1)} collective-permute-done((bf16[256,256]{1,0:T(8,128)(2,1)S(1)}, bf16[256,256]{1,0:T(8,128)(2,1)S(1)}, u32[]{:S(2)}, u32[]{:S(2)}) %collective-permute-start.2) | collective-permute-done | bytes 131104 | tf_op jit(solution)/shard_map/ppermute | solution.py:248
  32.8 1.3 %collective-permute-done.1.kv1 = bf16[256,256]{1,0:T(8,128)(2,1)S(1)} collective-permute-done((bf16[256,256]{1,0:T(8,128)(2,1)S(1)}, bf16[256,256]{1,0:T(8,128)(2,1)S(1)}, u32[]{:S(2)}, u32[]{:S(2)}) %collective-permute-start.1) | collective-permute-done | bytes 131104 | tf_op jit(solution)/shard_map/ppermute | solution.py:248
  34.1 0.5 collective-permute-done.kv0
  34.7 15.1 %attend.1 = (bf16[256,1024]{1,0:T(8,128)(2,1)}, bf16[256,256]{1,0:T(8,128)(2,1)S(1)}, bf16[256,256]{1,0:T(8,128)(2,1)S(1)}, bf16[256,256]{1,0:T(8,128)(2,1)S(1)}...) custom-call(bf16[256,2176]{1,0:T(8,128)(2,1)S(1)} %bitcast.5, bf16[256,256]{1,0:T(8,128)(2,1)S(1)} %collective-permute-done.kv0, ...), custom_call_target="tpu_custom_call" | custom-call | tf_op jit(solution)/shard_map/attend/pallas_call | solution.py:154
  49.8 0.7 copy-done
  50.5 2.8 %collective-permute-start.4 = (bf16[256,256]{1,0:T(8,128)(2,1)S(1)}, bf16[256,256]{1,0:T(8,128)(2,1)S(1)}, u32[]{:S(2)}, u32[]{:S(2)}) collective-permute-start(bf16[256,256]{1,0:T(8,128)(2,1)S(1)} %get-tuple-element.13), channel_id=1, source_target_pairs={{32,0},{33,1},{34,2},{35,3},{36,4},{37,5},{38,6},{39,7},{40,8},{41... | collective-permute-start | bytes 393224 | tf_op jit(solution)/shard_map/ppermute | solution.py:248
  53.3 3.8 %collective-permute-start.5 = (bf16[256,256]{1,0:T(8,128)(2,1)S(1)}, bf16[256,256]{1,0:T(8,128)(2,1)S(1)}, u32[]{:S(2)}, u32[]{:S(2)}) collective-permute-start(bf16[256,256]{1,0:T(8,128)(2,1)S(1)} %get-tuple-element.14), channel_id=1, source_target_pairs={{24,0},{25,1},{26,2},{27,3},{28,4},{29,5},{30,6},{31,7},{32,8},{33... | collective-permute-start | bytes 393224 | tf_op jit(solution)/shard_map/ppermute | solution.py:248
  57.2 2.5 %collective-permute-start.6 = (bf16[256,256]{1,0:T(8,128)(2,1)S(1)}, bf16[256,256]{1,0:T(8,128)(2,1)S(1)}, u32[]{:S(2)}, u32[]{:S(2)}) collective-permute-start(bf16[256,256]{1,0:T(8,128)(2,1)S(1)} %get-tuple-element.15), channel_id=1, source_target_pairs={{16,0},{17,1},{18,2},{19,3},{20,4},{21,5},{22,6},{23,7},{24,8},{25... | collective-permute-start | bytes 393224 | tf_op jit(solution)/shard_map/ppermute | solution.py:248
  59.7 2.1 %collective-permute-start.7 = (bf16[256,256]{1,0:T(8,128)(2,1)S(1)}, bf16[256,256]{1,0:T(8,128)(2,1)S(1)}, u32[]{:S(2)}, u32[]{:S(2)}) collective-permute-start(bf16[256,256]{1,0:T(8,128)(2,1)S(1)} %get-tuple-element.16), channel_id=1, source_target_pairs={{8,0},{9,1},{10,2},{11,3},{12,4},{13,5},{14,6},{15,7},{16,8},{17,9... | collective-permute-start | bytes 393224 | tf_op jit(solution)/shard_map/ppermute | solution.py:248
  61.9 0.4 collective-permute-done.5.ref2
  62.3 6.3 %collective-permute-done.6.ref3 = bf16[256,256]{1,0:T(8,128)(2,1)S(1)} collective-permute-done((bf16[256,256]{1,0:T(8,128)(2,1)S(1)}, bf16[256,256]{1,0:T(8,128)(2,1)S(1)}, u32[]{:S(2)}, u32[]{:S(2)}) %collective-permute-start.6) | collective-permute-done | bytes 131104 | tf_op jit(solution)/shard_map/ppermute | solution.py:248
  68.6 1.4 %collective-permute-done.7.ref4 = bf16[256,256]{1,0:T(8,128)(2,1)S(1)} collective-permute-done((bf16[256,256]{1,0:T(8,128)(2,1)S(1)}, bf16[256,256]{1,0:T(8,128)(2,1)S(1)}, u32[]{:S(2)}, u32[]{:S(2)}) %collective-permute-start.7) | collective-permute-done | bytes 131104 | tf_op jit(solution)/shard_map/ppermute | solution.py:248
  70.0 0.6 copy-done.6
  70.7 1.9 %add_parts.1 = bf16[256,256]{1,0:T(8,128)(2,1)} custom-call(f32[256,256]{1,0:T(8,128)} %copy-done, bf16[256,256]{1,0:T(8,128)(2,1)} %copy-done.3, bf16[256,256]{1,0:T(8,128)(2,1)} %copy-done.4, bf16[256,256]{1,0:T(8,128)(2,1)} %copy-done.5, bf16[256,256]{1,0:T(8,128)(2,1)} %copy-done.6), custom_call_target="tpu_custom_call" | custom-call | tf_op jit(solution)/shard_map/add_parts/pallas_call | solution.py:182
  72.5 10.8 %all_to_all.20.in_ref = bf16[8,32,256]{2,1,0:T(8,128)(2,1)} all-to-all(bf16[8,32,256]{2,1,0:T(8,128)(2,1)} %bitcast.12), channel_id=1, replica_groups={{0,1,2,3,4,5,6,7},{8,9,10,11,12,13,14,15},{16,17,18,19,20,21,22,23},{24..., dimensions={0} | all-to-all | bytes 262144 | tf_op jit(solution)/shard_map/all_to_all | solution.py:236
  83.4 3.5 %all-to-all-start.2 = ((bf16[8,32,1024]{2,1,0:T(8,128)(2,1)}), bf16[8,32,1024]{2,1,0:T(8,128)(2,1)S(1)}, u32[]{:S(2)}, u32[]{:S(2)}) async-start(bf16[8,32,1024]{2,1,0:T(8,128)(2,1)} %bitcast.3), calls=%async_computation.2 | async-start | bytes 1048576 | tf_op jit(solution)/shard_map/all_to_all | solution.py:236
  86.9 1.6 %unpack_keys.1 = (bf16[32,1024]{1,0:T(8,128)(2,1)}, bf16[32,1024]{1,0:T(8,128)(2,1)}) custom-call(bf16[8,32,256]{2,1,0:T(8,128)(2,1)} %all_to_all.20.in_ref), custom_call_target="tpu_custom_call" | custom-call | tf_op jit(solution)/shard_map/unpack_keys/pallas_call | solution.py:217
  88.5 8.7 %all-to-all-done.2.in_ref = bf16[8,32,1024]{2,1,0:T(8,128)(2,1)S(1)} async-done(((bf16[8,32,1024]{2,1,0:T(8,128)(2,1)}), bf16[8,32,1024]{2,1,0:T(8,128)(2,1)S(1)}, u32[]{:S(2)}, u32[]{:S(2)}) %all-to-all-start.2) | async-done | bytes 524320 | tf_op jit(solution)/shard_map/all_to_all | solution.py:236
  97.2 0.8 copy-done.1
  97.9 1.9 %unpack_queries.1 = bf16[32,8192]{1,0:T(8,128)(2,1)} custom-call(bf16[8,32,1024]{2,1,0:T(8,128)(2,1)} %copy-done.1), custom_call_target="tpu_custom_call" | custom-call | tf_op jit(solution)/shard_map/unpack_queries/pallas_call | solution.py:198
  (14 shorter events, 0.0 us)
Async XLA Ops:
  2.2 10.4 %all-to-all-start.1 = ((bf16[8,32,256]{2,1,0:T(8,128)(2,1)}), bf16[8,32,256]{2,1,0:T(8,128)(2,1)S(1)}, u32[]{:S(2)}, u32[]{:S(2)}) async-start(bf16[8,32,256]{2,1,0:T(8,128)(2,1)} %pack_keys.1), calls=%async_computation.1 | async-start | bytes 262144 | tf_op jit(solution)/shard_map/all_to_all | solution.py:236
  9.3 6.9 %copy-start.2 = (s32[16384]{0:T(1024)S(1)}, s32[16384]{0:T(1024)}, u32[]{:S(2)}) copy-start(s32[16384]{0:T(1024)} %param.11) | copy-start | bytes 196612
  12.6 22.1 %all-to-all-start = ((bf16[8,32,2176]{2,1,0:T(8,128)(2,1)}), bf16[8,32,2176]{2,1,0:T(8,128)(2,1)S(1)}, u32[]{:S(2)}, u32[]{:S(2)}) async-start(bf16[8,32,2176]{2,1,0:T(8,128)(2,1)} %pack_queries.1), calls=%async_computation | async-start | bytes 2228224 | tf_op jit(solution)/shard_map/all_to_all | solution.py:236
  16.3 14.7 %collective-permute-start.3 = (bf16[256,256]{1,0:T(8,128)(2,1)S(1)}, bf16[256,256]{1,0:T(8,128)(2,1)S(1)}, u32[]{:S(2)}, u32[]{:S(2)}) collective-permute-start(bf16[256,256]{1,0:T(8,128)(2,1)S(1)} %bitcast.6), channel_id=1, source_target_pairs={{0,8},{1,9},{2,10},{3,11},{4,12},{5,13},{6,14},{7,15},{8,16},{9,17... | collective-permute-start | bytes 393224 | tf_op jit(solution)/shard_map/ppermute | solution.py:248
  21.0 11.8 %collective-permute-start.2 = (bf16[256,256]{1,0:T(8,128)(2,1)S(1)}, bf16[256,256]{1,0:T(8,128)(2,1)S(1)}, u32[]{:S(2)}, u32[]{:S(2)}) collective-permute-start(bf16[256,256]{1,0:T(8,128)(2,1)S(1)} %bitcast.7), channel_id=1, source_target_pairs={{0,16},{1,17},{2,18},{3,19},{4,20},{5,21},{6,22},{7,23},{8,24},{9,... | collective-permute-start | bytes 393224 | tf_op jit(solution)/shard_map/ppermute | solution.py:248
  25.5 8.6 %collective-permute-start.1 = (bf16[256,256]{1,0:T(8,128)(2,1)S(1)}, bf16[256,256]{1,0:T(8,128)(2,1)S(1)}, u32[]{:S(2)}, u32[]{:S(2)}) collective-permute-start(bf16[256,256]{1,0:T(8,128)(2,1)S(1)} %bitcast.8), channel_id=1, source_target_pairs={{0,24},{1,25},{2,26},{3,27},{4,28},{5,29},{6,30},{7,31},{8,32},{9,... | collective-permute-start | bytes 393224 | tf_op jit(solution)/shard_map/ppermute | solution.py:248
  27.7 7.0 %collective-permute-start = (bf16[256,256]{1,0:T(8,128)(2,1)S(1)}, bf16[256,256]{1,0:T(8,128)(2,1)S(1)}, u32[]{:S(2)}, u32[]{:S(2)}) collective-permute-start(bf16[256,256]{1,0:T(8,128)(2,1)S(1)} %bitcast.9), channel_id=1, source_target_pairs={{0,32},{1,33},{2,34},{3,35},{4,36},{5,37},{6,38},{7,39},{8,40},{9,... | collective-permute-start | bytes 393224 | tf_op jit(solution)/shard_map/ppermute | solution.py:248
  49.8 0.7 copy-start
  50.5 11.4 %collective-permute-start.4 = (bf16[256,256]{1,0:T(8,128)(2,1)S(1)}, bf16[256,256]{1,0:T(8,128)(2,1)S(1)}, u32[]{:S(2)}, u32[]{:S(2)}) collective-permute-start(bf16[256,256]{1,0:T(8,128)(2,1)S(1)} %get-tuple-element.13), channel_id=1, source_target_pairs={{32,0},{33,1},{34,2},{35,3},{36,4},{37,5},{38,6},{39,7},{40,8},{41... | collective-permute-start | bytes 393224 | tf_op jit(solution)/shard_map/ppermute | solution.py:248
  53.3 9.0 %collective-permute-start.5 = (bf16[256,256]{1,0:T(8,128)(2,1)S(1)}, bf16[256,256]{1,0:T(8,128)(2,1)S(1)}, u32[]{:S(2)}, u32[]{:S(2)}) collective-permute-start(bf16[256,256]{1,0:T(8,128)(2,1)S(1)} %get-tuple-element.14), channel_id=1, source_target_pairs={{24,0},{25,1},{26,2},{27,3},{28,4},{29,5},{30,6},{31,7},{32,8},{33... | collective-permute-start | bytes 393224 | tf_op jit(solution)/shard_map/ppermute | solution.py:248
  57.2 11.4 %collective-permute-start.6 = (bf16[256,256]{1,0:T(8,128)(2,1)S(1)}, bf16[256,256]{1,0:T(8,128)(2,1)S(1)}, u32[]{:S(2)}, u32[]{:S(2)}) collective-permute-start(bf16[256,256]{1,0:T(8,128)(2,1)S(1)} %get-tuple-element.15), channel_id=1, source_target_pairs={{16,0},{17,1},{18,2},{19,3},{20,4},{21,5},{22,6},{23,7},{24,8},{25... | collective-permute-start | bytes 393224 | tf_op jit(solution)/shard_map/ppermute | solution.py:248
  59.7 10.3 %collective-permute-start.7 = (bf16[256,256]{1,0:T(8,128)(2,1)S(1)}, bf16[256,256]{1,0:T(8,128)(2,1)S(1)}, u32[]{:S(2)}, u32[]{:S(2)}) collective-permute-start(bf16[256,256]{1,0:T(8,128)(2,1)S(1)} %get-tuple-element.16), channel_id=1, source_target_pairs={{8,0},{9,1},{10,2},{11,3},{12,4},{13,5},{14,6},{15,7},{16,8},{17,9... | collective-permute-start | bytes 393224 | tf_op jit(solution)/shard_map/ppermute | solution.py:248
  61.9 8.1 %copy-start.3 = (bf16[256,256]{1,0:T(8,128)(2,1)}, bf16[256,256]{1,0:T(8,128)(2,1)S(1)}, u32[]{:S(2)}) copy-start(bf16[256,256]{1,0:T(8,128)(2,1)S(1)} %collective-permute-done.4.ref1) | copy-start | bytes 393220
  62.3 7.7 %copy-start.4 = (bf16[256,256]{1,0:T(8,128)(2,1)}, bf16[256,256]{1,0:T(8,128)(2,1)S(1)}, u32[]{:S(2)}) copy-start(bf16[256,256]{1,0:T(8,128)(2,1)S(1)} %collective-permute-done.5.ref2) | copy-start | bytes 393220
  68.6 1.4 %copy-start.5 = (bf16[256,256]{1,0:T(8,128)(2,1)}, bf16[256,256]{1,0:T(8,128)(2,1)S(1)}, u32[]{:S(2)}) copy-start(bf16[256,256]{1,0:T(8,128)(2,1)S(1)} %collective-permute-done.6.ref3) | copy-start | bytes 393220
  70.0 0.6 copy-start.6
  83.4 13.8 %all-to-all-start.2 = ((bf16[8,32,1024]{2,1,0:T(8,128)(2,1)}), bf16[8,32,1024]{2,1,0:T(8,128)(2,1)S(1)}, u32[]{:S(2)}, u32[]{:S(2)}) async-start(bf16[8,32,1024]{2,1,0:T(8,128)(2,1)} %bitcast.3), calls=%async_computation.2 | async-start | bytes 1048576 | tf_op jit(solution)/shard_map/all_to_all | solution.py:236
  97.2 0.8 copy-start.1

commit v2 on v1

--- a/solution.py
+++ b/solution.py
@@ -28,22 +28,10 @@
     )
 
 
-def pack_keys_kernel(key_ref, value_ref, out_ref):
-    for c in range(KEY_VALUE_HEADS):
-        columns = slice(c * HEAD_SIZE, (c + 1) * HEAD_SIZE)
-        out_ref[c, :, :HEAD_SIZE] = key_ref[:, columns]
-        out_ref[c, :, HEAD_SIZE:] = value_ref[:, columns]
-
-
 def pack_keys(keys, values):
     rows = keys.shape[0]
-    return pl.pallas_call(
-        pack_keys_kernel,
-        out_shape=jax.ShapeDtypeStruct((KEY_VALUE_HEADS, rows, 2 * HEAD_SIZE), jnp.bfloat16),
-        in_specs=[VMEM] * 2,
-        out_specs=VMEM,
-        name="pack_keys",
-    )(keys, values)
+    parts = [x.reshape(rows, KEY_VALUE_HEADS, HEAD_SIZE) for x in (keys, values)]
+    return jnp.concatenate(parts, axis=-1).transpose(1, 0, 2)
 
 
 def pack_queries_kernel(query_ref, out_ref, grad_ref, packed_ref):
@@ -108,40 +96,48 @@
     key_total[...] = jnp.zeros_like(key_total)
     value_total[...] = jnp.zeros_like(value_total)
 
-    def one_head(h, carry):
-        at = pl.multiple_of(h * HEAD_SIZE, HEAD_SIZE)
-        query = packed_ref[:, pl.ds(at, HEAD_SIZE)]
-        grad = packed_ref[:, pl.ds(COLUMNS + at, HEAD_SIZE)]
-        row_delta = delta[pl.ds(h, 1), :]
-        largest = jnp.full((1, block), -jnp.inf, jnp.float32)
-        for j in range(parts):
-            part = contract_last(kv[j][:, :HEAD_SIZE], query) * (SCALE * LOG2E) + bias[rows[j], :]
-            scores[rows[j], :] = part
-            largest = jnp.maximum(largest, jnp.max(part, axis=0, keepdims=True))
-        total = jnp.zeros((1, block), jnp.float32)
-        for j in range(parts):
-            part = jnp.exp2(scores[rows[j], :] - largest)
-            scores[rows[j], :] = part
-            total = total + jnp.sum(part, axis=0, keepdims=True)
+    sub = 256
+    pieces = block * parts // sub
+    spans = [slice(i * sub, (i + 1) * sub) for i in range(pieces)]
+    group = 4
+    wide = group * block
+    def kvs(i, columns):
+        j, o = divmod(i * sub, block)
+        return kv[j][o : o + sub, columns]
+    for g in range(HEADS_EACH // group):
+        heads = range(g * group, (g + 1) * group)
+        query = jnp.concatenate([packed_ref[:, h * HEAD_SIZE : (h + 1) * HEAD_SIZE] for h in heads], axis=0)
+        grad = jnp.concatenate([packed_ref[:, COLUMNS + h * HEAD_SIZE : COLUMNS + (h + 1) * HEAD_SIZE] for h in heads], axis=0)
+        row_delta = jnp.concatenate([delta[h : h + 1, :] for h in heads], axis=1)
+        tops, sums = [], []
+        for i in range(pieces):
+            b = bias[spans[i], :]
+            if group > 1:
+                b = jnp.concatenate([b] * group, axis=1)
+            part = contract_last(kvs(i, slice(0, HEAD_SIZE)), query) * (SCALE * LOG2E) + b
+            top = jnp.max(part, axis=0, keepdims=True)
+            part = jnp.exp2(part - top)
+            scores[spans[i], :] = part.astype(scores.dtype)
+            tops.append(top)
+            sums.append(jnp.sum(part, axis=0, keepdims=True))
+        largest = tops[0]
+        for top in tops[1:]:
+            largest = jnp.maximum(largest, top)
+        factors = [jnp.exp2(top - largest) for top in tops]
+        total = factors[0] * sums[0]
+        for f, s in zip(factors[1:], sums[1:]):
+            total = total + f * s
         inverse = 1.0 / total
-        query_grad = jnp.zeros((HEAD_SIZE, block), jnp.float32)
-        for j in range(parts):
-            probs = scores[rows[j], :] * inverse
-            value_total[rows[j], :] += jnp.dot(
-                probs.astype(jnp.bfloat16), grad, preferred_element_type=jnp.float32
-            )
-            grad_probs = contract_last(kv[j][:, HEAD_SIZE:], grad)
+        query_grad = jnp.zeros((HEAD_SIZE, wide), jnp.float32)
+        for i in range(pieces):
+            probs = scores[spans[i], :].astype(jnp.float32) * (factors[i] * inverse)
+            value_total[spans[i], :] += jnp.dot(probs.astype(jnp.bfloat16), grad, preferred_element_type=jnp.float32)
+            grad_probs = contract_last(kvs(i, slice(HEAD_SIZE, 2 * HEAD_SIZE)), grad)
             grad_scores = (probs * (grad_probs - row_delta)).astype(jnp.bfloat16)
-            key_total[rows[j], :] += jnp.dot(
-                grad_scores, query, preferred_element_type=jnp.float32
-            )
-            query_grad = query_grad + jnp.dot(
-                key_turned[:, rows[j]], grad_scores, preferred_element_type=jnp.float32
-            )
-        grad_query_ref[:, pl.ds(at, HEAD_SIZE)] = (query_grad * SCALE).T.astype(jnp.bfloat16)
-        return carry
-
-    lax.fori_loop(0, HEADS_EACH, one_head, 0)
+            key_total[spans[i], :] += jnp.dot(grad_scores, query, preferred_element_type=jnp.float32)
+            query_grad = query_grad + jnp.dot(key_turned[:, spans[i]], grad_scores, preferred_element_type=jnp.float32)
+        for n, h in enumerate(heads):
+            grad_query_ref[:, h * HEAD_SIZE : (h + 1) * HEAD_SIZE] = (query_grad[:, n * block : (n + 1) * block] * SCALE).T.astype(jnp.bfloat16)
     for j in range(parts):
         outs[j][:, :HEAD_SIZE] = (key_total[rows[j], :] * SCALE).astype(outs[j].dtype)
         outs[j][:, HEAD_SIZE:] = value_total[rows[j], :].astype(outs[j].dtype)
@@ -161,7 +157,7 @@
         scratch_shapes=[
             pltpu.VMEM((keys, block), jnp.float32),
             pltpu.VMEM((HEAD_SIZE, keys), jnp.bfloat16),
-            pltpu.VMEM((keys, block), jnp.float32),
+            pltpu.VMEM((keys, 4 * block), jnp.float32),
             pltpu.VMEM((HEADS_EACH, block), jnp.float32),
             pltpu.VMEM((keys, HEAD_SIZE), jnp.float32),
             pltpu.VMEM((keys, HEAD_SIZE), jnp.float32),
@@ -171,21 +167,10 @@
     )(packed, *kv, first)
 
 
-def add_kernel(own_ref, ref1, ref2, ref3, ref4, out_ref):
-    total = own_ref[...]
-    for ref in (ref1, ref2, ref3, ref4):
-        total = total + ref[...].astype(jnp.float32)
-    out_ref[...] = total.astype(jnp.bfloat16)
-
-
 def add_parts(own, others):
-    return pl.pallas_call(
-        add_kernel,
-        out_shape=jax.ShapeDtypeStruct(own.shape, jnp.bfloat16),
-        in_specs=[VMEM] * (1 + len(others)),
-        out_specs=VMEM,
-        name="add_parts",
-    )(own, *others)
+    for other in others:
+        own = own + other.astype(jnp.float32)
+    return own.astype(jnp.bfloat16)
 
 
 def unpack_queries_kernel(in_ref, out_ref):
@@ -204,23 +189,13 @@
     )(packed)
 
 
-def unpack_keys_kernel(in_ref, key_ref, value_ref):
-    for c in range(KEY_VALUE_HEADS):
-        columns = slice(c * HEAD_SIZE, (c + 1) * HEAD_SIZE)
-        key_ref[:, columns] = in_ref[c, :, :HEAD_SIZE]
-        value_ref[:, columns] = in_ref[c, :, HEAD_SIZE:]
-
-
 def unpack_keys(packed):
     rows = packed.shape[1]
-    shape = jax.ShapeDtypeStruct((rows, KEY_VALUE_HEADS * HEAD_SIZE), jnp.bfloat16)
-    return pl.pallas_call(
-        unpack_keys_kernel,
-        out_shape=[shape, shape],
-        in_specs=[VMEM],
-        out_specs=[VMEM] * 2,
-        name="unpack_keys",
-    )(packed)
+    packed = packed.transpose(1, 0, 2)
+    return tuple(
+        packed[:, :, i * HEAD_SIZE : (i + 1) * HEAD_SIZE].reshape(rows, KEY_VALUE_HEADS * HEAD_SIZE)
+        for i in range(2)
+    )
 
 
 def on_device(queries, key_state_rows, value_state_rows, attn_output, grad_output, doc_ids):
@@ -261,6 +236,7 @@
     grad_rows = exchange(grad_query.reshape(sharers, rows, COLUMNS))
     others = [shift(grad_kv[j], j - BEHIND) for j in range(BEHIND)]
     grad_own = add_parts(grad_kv[BEHIND], others)
+    grad_own, grad_rows = lax.optimization_barrier((grad_own, grad_rows))
     kv_rows = exchange(grad_own.reshape(sharers, rows, 2 * HEAD_SIZE))
     key_state_gradient, value_state_gradient = unpack_keys(kv_rows)
     return unpack_queries(grad_rows), key_state_gradient, value_state_gradient

time: 101 us -> 83.6 us (0.83)
  Pallas kernels: 24.8 us -> 13.9 us
  blocking collectives: 10.8 us -> 0 us
  starting transfers between devices: 37 us -> 42.6 us
  waiting for transfers between devices: 23.8 us -> 20.6 us
  other arithmetic: 0.25 us -> 1.64 us
    all_to_all x1 -> x0, blocking collectives: 10.8 us -> none  [exchange(): lax.all_to_all(value, 'head', split_axis=0, concat_axis=0, axis_index_gro...]
    pallas_call x1, Pallas kernels: 15.1 us -> 9.24 us  [attend(): pl.pallas_call(attend_kernel, out_shape=[jax.ShapeDtypeStruct((block, COL...]
    all_to_all x3 -> x4, starting transfers between devices: 11.4 us -> 16.9 us  [exchange(): lax.all_to_all(value, 'head', split_axis=0, concat_axis=0, axis_index_gro...]
    pallas_call x3 -> x0, Pallas kernels: 5.01 us -> none  [the longest x1 1.88 us: add_parts(): pl.pallas_call(add_kernel, out_shape=jax.ShapeDtypeStruct(own.shape, jnp....]
    all_to_all x3 -> x4, waiting for transfers between devices: 12 us -> 7.57 us  [exchange(): lax.all_to_all(value, 'head', split_axis=0, concat_axis=0, axis_index_gro...]
    reshape x0 -> x3, local copies, waits for them, and re-layouts: none -> 2.14 us  [the longest x2 1.28 us: unpack_keys(): packed[:, :, i * HEAD_SIZE:(i + 1) * HEAD_SIZE]]
    unnamed x14 -> x7, local copies, waits for them, and re-layouts: 2.14 us -> 0.87 us
    ppermute x8, waiting for transfers between devices: 11.8 us -> 13 us  [shift(): return lax.ppermute(value, ('ctx', 'head'), pairs)]
  transfers between devices with their start and end apart: 11 -> 12, of which waited for: 8 -> 8; matrix products, arithmetic and copies ran while one was open for 0% -> 1% of each run, Pallas kernels for 4% -> 6%
where the time goes in v2:
time: 83.6 us; the launch traced here: 82.8 us
  starting transfers between devices  42.6 us (51%)
  waiting for transfers between devices  20.6 us (25%)
  Pallas kernels  13.9 us (17%)
  local copies, waits for them, and re-layouts  3.18 us (4%)
  other arithmetic  1.64 us (2%)
    ppermute x8, starting transfers between devices, shift(): return lax.ppermute(value, ('ctx', 'head'), pairs)  25.8 us
    all_to_all x4, starting transfers between devices, exchange(): lax.all_to_all(value, 'head', split_axis=0, concat_axis=0, axis_index_gro...  16.9 us
    ppermute x8, waiting for transfers between devices, shift(): return lax.ppermute(value, ('ctx', 'head'), pairs)  13 us
    pallas_call x1, Pallas kernels, attend(): pl.pallas_call(attend_kernel, out_shape=[jax.ShapeDtypeStruct((block, COL...  9.24 us
    all_to_all x4, waiting for transfers between devices, exchange(): lax.all_to_all(value, 'head', split_axis=0, concat_axis=0, axis_index_gro...  7.57 us
    pallas_call x1, Pallas kernels, pack_queries(): pl.pallas_call(pack_queries_kernel, out_shape=jax.ShapeDtypeStruct((KEY_V...  2.83 us
    pallas_call x1, Pallas kernels, unpack_queries(): pl.pallas_call(unpack_queries_kernel, out_shape=jax.ShapeDtypeStruct((row...  1.87 us
  transfers between devices with their start and end apart: 12, of which 8 were waited for; matrix products, arithmetic and copies ran while one was open for 1% of the time, Pallas kernels for 6%

profile of v2, /device:TPU:248, one launch (start us, length us, event | category | flops | bytes accessed | tf_op | source)
XLA Modules:
  0.0 82.8 jit_solution(5654485387010595332)
XLA Ops:
  0.6 0.8 %copy-done = bf16[32,1024]{1,0:T(8,128)(2,1)S(1)} copy-done((bf16[32,1024]{1,0:T(8,128)(2,1)S(1)}, bf16[32,1024]{1,0:T(8,128)(2,1)}, u32[]{:S(2)}) %copy-start) | copy-done | bytes 65560
  1.5 0.9 %copy_bitcast_fusion.2 = (bf16[32,8,128]{2,0,1:T(8,128)(2,1)S(1)}, bf16[32,8,128]{2,0,1:T(8,128)(2,1)S(1)}) fusion(bf16[32,1024]{1,0:T(8,128)(2,1)S(1)} %copy-done, bf16[32,1024]{1,0:T(8,128)(2,1)} %param.8), kind=kLoop, calls=%fused_computation.7 | loop fusion | bytes 262144 | tf_op jit(solution)/shard_map/reshape | solution.py:33
  2.3 0.7 maximum_bitcast_fusion
  3.0 4.3 %all-to-all-start.1 = ((bf16[8,32,256]{2,1,0:T(8,128)(2,1)}), bf16[8,32,256]{2,1,0:T(8,128)(2,1)S(1)}, u32[]{:S(2)}, u32[]{:S(2)}) async-start(bf16[8,32,256]{2,1,0:T(8,128)(2,1)} %maximum_bitcast_fusion), calls=%async_computation.1 | async-start | bytes 262144 | tf_op jit(solution)/shard_map/all_to_all | solution.py:211
  7.3 2.8 %pack_queries.1 = bf16[8,32,2176]{2,1,0:T(8,128)(2,1)} custom-call(bf16[32,8192]{1,0:T(8,128)(2,1)} %query_ref.1, bf16[32,8192]{1,0:T(8,128)(2,1)} %out_ref.1, bf16[32,8192]{1,0:T(8,128)(2,1)} %grad_ref.1), custom_call_target="tpu_custom_call" | custom-call | tf_op jit(solution)/shard_map/pack_queries/pallas_call | solution.py:63
  10.1 3.3 %all-to-all-done.1 = bf16[8,32,256]{2,1,0:T(8,128)(2,1)S(1)} async-done(((bf16[8,32,256]{2,1,0:T(8,128)(2,1)}), bf16[8,32,256]{2,1,0:T(8,128)(2,1)S(1)}, u32[]{:S(2)}, u32[]{:S(2)}) %all-to-all-start.1) | async-done | bytes 131104 | tf_op jit(solution)/shard_map/all_to_all | solution.py:211
  13.5 3.6 %all-to-all-start = ((bf16[8,32,2176]{2,1,0:T(8,128)(2,1)}), bf16[8,32,2176]{2,1,0:T(8,128)(2,1)S(1)}, u32[]{:S(2)}, u32[]{:S(2)}) async-start(bf16[8,32,2176]{2,1,0:T(8,128)(2,1)} %pack_queries.1), calls=%async_computation | async-start | bytes 2228224 | tf_op jit(solution)/shard_map/all_to_all | solution.py:211
  17.1 0.1 pad_dynamic-slice_fusion.1
  17.1 4.7 %collective-permute-start.3 = (bf16[256,256]{1,0:T(8,128)(2,1)S(1)}, bf16[256,256]{1,0:T(8,128)(2,1)S(1)}, u32[]{:S(2)}, u32[]{:S(2)}) collective-permute-start(bf16[256,256]{1,0:T(8,128)(2,1)S(1)} %bitcast.29), channel_id=1, source_target_pairs={{0,8},{1,9},{2,10},{3,11},{4,12},{5,13},{6,14},{7,15},{8,16},{9,17... | collective-permute-start | bytes 393224 | tf_op jit(solution)/shard_map/ppermute | solution.py:223
  21.8 4.5 %collective-permute-start.2 = (bf16[256,256]{1,0:T(8,128)(2,1)S(1)}, bf16[256,256]{1,0:T(8,128)(2,1)S(1)}, u32[]{:S(2)}, u32[]{:S(2)}) collective-permute-start(bf16[256,256]{1,0:T(8,128)(2,1)S(1)} %bitcast.30), channel_id=1, source_target_pairs={{0,16},{1,17},{2,18},{3,19},{4,20},{5,21},{6,22},{7,23},{8,24},{9,... | collective-permute-start | bytes 393224 | tf_op jit(solution)/shard_map/ppermute | solution.py:223
  26.3 2.2 %collective-permute-start.1 = (bf16[256,256]{1,0:T(8,128)(2,1)S(1)}, bf16[256,256]{1,0:T(8,128)(2,1)S(1)}, u32[]{:S(2)}, u32[]{:S(2)}) collective-permute-start(bf16[256,256]{1,0:T(8,128)(2,1)S(1)} %bitcast.31), channel_id=1, source_target_pairs={{0,24},{1,25},{2,26},{3,27},{4,28},{5,29},{6,30},{7,31},{8,32},{9,... | collective-permute-start | bytes 393224 | tf_op jit(solution)/shard_map/ppermute | solution.py:223
  28.6 2.9 %collective-permute-start = (bf16[256,256]{1,0:T(8,128)(2,1)S(1)}, bf16[256,256]{1,0:T(8,128)(2,1)S(1)}, u32[]{:S(2)}, u32[]{:S(2)}) collective-permute-start(bf16[256,256]{1,0:T(8,128)(2,1)S(1)} %bitcast.32), channel_id=1, source_target_pairs={{0,32},{1,33},{2,34},{3,35},{4,36},{5,37},{6,38},{7,39},{8,40},{9,... | collective-permute-start | bytes 393224 | tf_op jit(solution)/shard_map/ppermute | solution.py:223
  31.5 0.1 pad_dynamic-slice_fusion
  31.6 0.2 convert_reduce_fusion
  31.8 1.8 %collective-permute-done.2.kv2 = bf16[256,256]{1,0:T(8,128)(2,1)S(1)} collective-permute-done((bf16[256,256]{1,0:T(8,128)(2,1)S(1)}, bf16[256,256]{1,0:T(8,128)(2,1)S(1)}, u32[]{:S(2)}, u32[]{:S(2)}) %collective-permute-start.2) | collective-permute-done | bytes 131104 | tf_op jit(solution)/shard_map/ppermute | solution.py:223
  33.6 1.3 %collective-permute-done.1.kv1 = bf16[256,256]{1,0:T(8,128)(2,1)S(1)} collective-permute-done((bf16[256,256]{1,0:T(8,128)(2,1)S(1)}, bf16[256,256]{1,0:T(8,128)(2,1)S(1)}, u32[]{:S(2)}, u32[]{:S(2)}) %collective-permute-start.1) | collective-permute-done | bytes 131104 | tf_op jit(solution)/shard_map/ppermute | solution.py:223
  35.0 0.5 collective-permute-done.kv0
  35.5 9.2 %attend.1 = (bf16[256,1024]{1,0:T(8,128)(2,1)}, bf16[256,256]{1,0:T(8,128)(2,1)S(1)}, bf16[256,256]{1,0:T(8,128)(2,1)S(1)}, bf16[256,256]{1,0:T(8,128)(2,1)S(1)}...) custom-call(bf16[256,2176]{1,0:T(8,128)(2,1)S(1)} %bitcast.28, bf16[256,256]{1,0:T(8,128)(2,1)S(1)} %collective-permute-done.kv0, ...), custom_call_target="tpu_custom_call" | custom-call | tf_op jit(solution)/shard_map/attend/pallas_call | solution.py:150
  44.8 4.6 %all-to-all-start.2 = ((bf16[8,32,1024]{2,1,0:T(8,128)(2,1)}), bf16[8,32,1024]{2,1,0:T(8,128)(2,1)S(1)}, u32[]{:S(2)}, u32[]{:S(2)}) async-start(bf16[8,32,1024]{2,1,0:T(8,128)(2,1)} %bitcast.4), calls=%async_computation.2 | async-start | bytes 1048576 | tf_op jit(solution)/shard_map/all_to_all | solution.py:211
  49.3 2.9 %collective-permute-start.4 = (bf16[256,256]{1,0:T(8,128)(2,1)S(1)}, bf16[256,256]{1,0:T(8,128)(2,1)S(1)}, u32[]{:S(2)}, u32[]{:S(2)}) collective-permute-start(bf16[256,256]{1,0:T(8,128)(2,1)S(1)} %get-tuple-element.12), channel_id=1, source_target_pairs={{32,0},{33,1},{34,2},{35,3},{36,4},{37,5},{38,6},{39,7},{40,8},{41... | collective-permute-start | bytes 393224 | tf_op jit(solution)/shard_map/ppermute | solution.py:223
  52.2 3.9 %collective-permute-start.5 = (bf16[256,256]{1,0:T(8,128)(2,1)S(1)}, bf16[256,256]{1,0:T(8,128)(2,1)S(1)}, u32[]{:S(2)}, u32[]{:S(2)}) collective-permute-start(bf16[256,256]{1,0:T(8,128)(2,1)S(1)} %get-tuple-element.13), channel_id=1, source_target_pairs={{24,0},{25,1},{26,2},{27,3},{28,4},{29,5},{30,6},{31,7},{32,8},{33... | collective-permute-start | bytes 393224 | tf_op jit(solution)/shard_map/ppermute | solution.py:223
  56.1 2.5 %collective-permute-start.6 = (bf16[256,256]{1,0:T(8,128)(2,1)S(1)}, bf16[256,256]{1,0:T(8,128)(2,1)S(1)}, u32[]{:S(2)}, u32[]{:S(2)}) collective-permute-start(bf16[256,256]{1,0:T(8,128)(2,1)S(1)} %get-tuple-element.14), channel_id=1, source_target_pairs={{16,0},{17,1},{18,2},{19,3},{20,4},{21,5},{22,6},{23,7},{24,8},{25... | collective-permute-start | bytes 393224 | tf_op jit(solution)/shard_map/ppermute | solution.py:223
  58.6 2.2 %collective-permute-start.7 = (bf16[256,256]{1,0:T(8,128)(2,1)S(1)}, bf16[256,256]{1,0:T(8,128)(2,1)S(1)}, u32[]{:S(2)}, u32[]{:S(2)}) collective-permute-start(bf16[256,256]{1,0:T(8,128)(2,1)S(1)} %get-tuple-element.15), channel_id=1, source_target_pairs={{8,0},{9,1},{10,2},{11,3},{12,4},{13,5},{14,6},{15,7},{16,8},{17,9... | collective-permute-start | bytes 393224 | tf_op jit(solution)/shard_map/ppermute | solution.py:223
  60.8 1.2 %collective-permute-done.5 = bf16[256,256]{1,0:T(8,128)(2,1)S(1)} collective-permute-done((bf16[256,256]{1,0:T(8,128)(2,1)S(1)}, bf16[256,256]{1,0:T(8,128)(2,1)S(1)}, u32[]{:S(2)}, u32[]{:S(2)}) %collective-permute-start.5) | collective-permute-done | bytes 131104 | tf_op jit(solution)/shard_map/ppermute | solution.py:223
  62.0 6.3 %collective-permute-done.6 = bf16[256,256]{1,0:T(8,128)(2,1)S(1)} collective-permute-done((bf16[256,256]{1,0:T(8,128)(2,1)S(1)}, bf16[256,256]{1,0:T(8,128)(2,1)S(1)}, u32[]{:S(2)}, u32[]{:S(2)}) %collective-permute-start.6) | collective-permute-done | bytes 131104 | tf_op jit(solution)/shard_map/ppermute | solution.py:223
  68.3 1.9 %collective-permute-done.7 = bf16[256,256]{1,0:T(8,128)(2,1)S(1)} collective-permute-done((bf16[256,256]{1,0:T(8,128)(2,1)S(1)}, bf16[256,256]{1,0:T(8,128)(2,1)S(1)}, u32[]{:S(2)}, u32[]{:S(2)}) %collective-permute-start.7) | collective-permute-done | bytes 131104 | tf_op jit(solution)/shard_map/ppermute | solution.py:223
  70.2 0.7 add_convert_fusion
  70.9 4.4 %all-to-all-start.3 = ((bf16[8,32,256]{2,1,0:T(8,128)(2,1)}), bf16[8,32,256]{2,1,0:T(8,128)(2,1)S(1)}, u32[]{:S(2)}, u32[]{:S(2)}) async-start(bf16[8,32,256]{2,1,0:T(8,128)(2,1)} %bitcast.5), calls=%async_computation.3 | async-start | bytes 262144 | tf_op jit(solution)/shard_map/all_to_all | solution.py:211
  75.3 1.9 %unpack_queries.1 = bf16[32,8192]{1,0:T(8,128)(2,1)} custom-call(bf16[8,32,1024]{2,1,0:T(8,128)(2,1)} %copy-done.1), custom_call_target="tpu_custom_call" | custom-call | tf_op jit(solution)/shard_map/unpack_queries/pallas_call | solution.py:183
  77.2 4.3 %all-to-all-done.3 = bf16[8,32,256]{2,1,0:T(8,128)(2,1)S(1)} async-done(((bf16[8,32,256]{2,1,0:T(8,128)(2,1)}), bf16[8,32,256]{2,1,0:T(8,128)(2,1)S(1)}, u32[]{:S(2)}, u32[]{:S(2)}) %all-to-all-start.3) | async-done | bytes 131104 | tf_op jit(solution)/shard_map/all_to_all | solution.py:211
  81.5 0.6 copy.25
  82.1 0.6 copy.26
  (10 shorter events, 0.0 us)
Async XLA Ops:
  0.6 0.8 %copy-start = (bf16[32,1024]{1,0:T(8,128)(2,1)S(1)}, bf16[32,1024]{1,0:T(8,128)(2,1)}, u32[]{:S(2)}) copy-start(bf16[32,1024]{1,0:T(8,128)(2,1)} %param.7) | copy-start | bytes 196612
  3.0 10.4 %all-to-all-start.1 = ((bf16[8,32,256]{2,1,0:T(8,128)(2,1)}), bf16[8,32,256]{2,1,0:T(8,128)(2,1)S(1)}, u32[]{:S(2)}, u32[]{:S(2)}) async-start(bf16[8,32,256]{2,1,0:T(8,128)(2,1)} %maximum_bitcast_fusion), calls=%async_computation.1 | async-start | bytes 262144 | tf_op jit(solution)/shard_map/all_to_all | solution.py:211
  10.1 6.9 %copy-start.2 = (s32[16384]{0:T(1024)S(1)}, s32[16384]{0:T(1024)}, u32[]{:S(2)}) copy-start(s32[16384]{0:T(1024)} %param.11) | copy-start | bytes 196612
  13.5 22.1 %all-to-all-start = ((bf16[8,32,2176]{2,1,0:T(8,128)(2,1)}), bf16[8,32,2176]{2,1,0:T(8,128)(2,1)S(1)}, u32[]{:S(2)}, u32[]{:S(2)}) async-start(bf16[8,32,2176]{2,1,0:T(8,128)(2,1)} %pack_queries.1), calls=%async_computation | async-start | bytes 2228224 | tf_op jit(solution)/shard_map/all_to_all | solution.py:211
  17.1 14.7 %collective-permute-start.3 = (bf16[256,256]{1,0:T(8,128)(2,1)S(1)}, bf16[256,256]{1,0:T(8,128)(2,1)S(1)}, u32[]{:S(2)}, u32[]{:S(2)}) collective-permute-start(bf16[256,256]{1,0:T(8,128)(2,1)S(1)} %bitcast.29), channel_id=1, source_target_pairs={{0,8},{1,9},{2,10},{3,11},{4,12},{5,13},{6,14},{7,15},{8,16},{9,17... | collective-permute-start | bytes 393224 | tf_op jit(solution)/shard_map/ppermute | solution.py:223
  21.8 11.8 %collective-permute-start.2 = (bf16[256,256]{1,0:T(8,128)(2,1)S(1)}, bf16[256,256]{1,0:T(8,128)(2,1)S(1)}, u32[]{:S(2)}, u32[]{:S(2)}) collective-permute-start(bf16[256,256]{1,0:T(8,128)(2,1)S(1)} %bitcast.30), channel_id=1, source_target_pairs={{0,16},{1,17},{2,18},{3,19},{4,20},{5,21},{6,22},{7,23},{8,24},{9,... | collective-permute-start | bytes 393224 | tf_op jit(solution)/shard_map/ppermute | solution.py:223
  26.3 8.6 %collective-permute-start.1 = (bf16[256,256]{1,0:T(8,128)(2,1)S(1)}, bf16[256,256]{1,0:T(8,128)(2,1)S(1)}, u32[]{:S(2)}, u32[]{:S(2)}) collective-permute-start(bf16[256,256]{1,0:T(8,128)(2,1)S(1)} %bitcast.31), channel_id=1, source_target_pairs={{0,24},{1,25},{2,26},{3,27},{4,28},{5,29},{6,30},{7,31},{8,32},{9,... | collective-permute-start | bytes 393224 | tf_op jit(solution)/shard_map/ppermute | solution.py:223
  28.6 7.0 %collective-permute-start = (bf16[256,256]{1,0:T(8,128)(2,1)S(1)}, bf16[256,256]{1,0:T(8,128)(2,1)S(1)}, u32[]{:S(2)}, u32[]{:S(2)}) collective-permute-start(bf16[256,256]{1,0:T(8,128)(2,1)S(1)} %bitcast.32), channel_id=1, source_target_pairs={{0,32},{1,33},{2,34},{3,35},{4,36},{5,37},{6,38},{7,39},{8,40},{9,... | collective-permute-start | bytes 393224 | tf_op jit(solution)/shard_map/ppermute | solution.py:223
  44.8 26.1 %all-to-all-start.2 = ((bf16[8,32,1024]{2,1,0:T(8,128)(2,1)}), bf16[8,32,1024]{2,1,0:T(8,128)(2,1)S(1)}, u32[]{:S(2)}, u32[]{:S(2)}) async-start(bf16[8,32,1024]{2,1,0:T(8,128)(2,1)} %bitcast.4), calls=%async_computation.2 | async-start | bytes 1048576 | tf_op jit(solution)/shard_map/all_to_all | solution.py:211
  49.3 11.5 %collective-permute-start.4 = (bf16[256,256]{1,0:T(8,128)(2,1)S(1)}, bf16[256,256]{1,0:T(8,128)(2,1)S(1)}, u32[]{:S(2)}, u32[]{:S(2)}) collective-permute-start(bf16[256,256]{1,0:T(8,128)(2,1)S(1)} %get-tuple-element.12), channel_id=1, source_target_pairs={{32,0},{33,1},{34,2},{35,3},{36,4},{37,5},{38,6},{39,7},{40,8},{41... | collective-permute-start | bytes 393224 | tf_op jit(solution)/shard_map/ppermute | solution.py:223
  52.2 9.7 %collective-permute-start.5 = (bf16[256,256]{1,0:T(8,128)(2,1)S(1)}, bf16[256,256]{1,0:T(8,128)(2,1)S(1)}, u32[]{:S(2)}, u32[]{:S(2)}) collective-permute-start(bf16[256,256]{1,0:T(8,128)(2,1)S(1)} %get-tuple-element.13), channel_id=1, source_target_pairs={{24,0},{25,1},{26,2},{27,3},{28,4},{29,5},{30,6},{31,7},{32,8},{33... | collective-permute-start | bytes 393224 | tf_op jit(solution)/shard_map/ppermute | solution.py:223
  56.1 12.2 %collective-permute-start.6 = (bf16[256,256]{1,0:T(8,128)(2,1)S(1)}, bf16[256,256]{1,0:T(8,128)(2,1)S(1)}, u32[]{:S(2)}, u32[]{:S(2)}) collective-permute-start(bf16[256,256]{1,0:T(8,128)(2,1)S(1)} %get-tuple-element.14), channel_id=1, source_target_pairs={{16,0},{17,1},{18,2},{19,3},{20,4},{21,5},{22,6},{23,7},{24,8},{25... | collective-permute-start | bytes 393224 | tf_op jit(solution)/shard_map/ppermute | solution.py:223
  58.6 11.5 %collective-permute-start.7 = (bf16[256,256]{1,0:T(8,128)(2,1)S(1)}, bf16[256,256]{1,0:T(8,128)(2,1)S(1)}, u32[]{:S(2)}, u32[]{:S(2)}) collective-permute-start(bf16[256,256]{1,0:T(8,128)(2,1)S(1)} %get-tuple-element.15), channel_id=1, source_target_pairs={{8,0},{9,1},{10,2},{11,3},{12,4},{13,5},{14,6},{15,7},{16,8},{17,9... | collective-permute-start | bytes 393224 | tf_op jit(solution)/shard_map/ppermute | solution.py:223
  70.9 4.5 %copy-start.1 = (bf16[8,32,1024]{2,1,0:T(8,128)(2,1)}, bf16[8,32,1024]{2,1,0:T(8,128)(2,1)S(1)}, u32[]{:S(2)}) copy-start(bf16[8,32,1024]{2,1,0:T(8,128)(2,1)S(1)} %all-to-all-done.2.in_ref) | copy-start | bytes 1572868
  70.9 10.6 %all-to-all-start.3 = ((bf16[8,32,256]{2,1,0:T(8,128)(2,1)}), bf16[8,32,256]{2,1,0:T(8,128)(2,1)S(1)}, u32[]{:S(2)}, u32[]{:S(2)}) async-start(bf16[8,32,256]{2,1,0:T(8,128)(2,1)} %bitcast.5), calls=%async_computation.3 | async-start | bytes 262144 | tf_op jit(solution)/shard_map/all_to_all | solution.py:211

commit v3 on v2

--- a/solution.py
+++ b/solution.py
@@ -28,10 +28,22 @@
     )
 
 
+def pack_keys_kernel(key_ref, value_ref, out_ref):
+    for c in range(KEY_VALUE_HEADS):
+        columns = slice(c * HEAD_SIZE, (c + 1) * HEAD_SIZE)
+        out_ref[c, :, :HEAD_SIZE] = key_ref[:, columns]
+        out_ref[c, :, HEAD_SIZE:] = value_ref[:, columns]
+
+
 def pack_keys(keys, values):
     rows = keys.shape[0]
-    parts = [x.reshape(rows, KEY_VALUE_HEADS, HEAD_SIZE) for x in (keys, values)]
-    return jnp.concatenate(parts, axis=-1).transpose(1, 0, 2)
+    return pl.pallas_call(
+        pack_keys_kernel,
+        out_shape=jax.ShapeDtypeStruct((KEY_VALUE_HEADS, rows, 2 * HEAD_SIZE), jnp.bfloat16),
+        in_specs=[VMEM] * 2,
+        out_specs=VMEM,
+        name="pack_keys",
+    )(keys, values)
 
 
 def pack_queries_kernel(query_ref, out_ref, grad_ref, packed_ref):
@@ -74,12 +86,13 @@
 def attend_kernel(
     packed_ref, kv0, kv1, kv2, kv3, kv4, first_ref,
     grad_query_ref, out0, out1, out2, out3, out4,
-    bias, key_turned, scores, delta, key_total, value_total,
+    bias, keys_ref, values_ref, key_turned,
 ):
     kv = (kv0, kv1, kv2, kv3, kv4)
     outs = (out0, out1, out2, out3, out4)
     block = kv0.shape[0]
     parts = len(kv)
+    heads = range(HEADS_EACH)
     rows = [slice(j * block, (j + 1) * block) for j in range(parts)]
     first = first_ref[...]
     last = lax.broadcasted_iota(jnp.int32, (1, block), 1) + (parts - 1) * block
@@ -87,60 +100,37 @@
         key_at = lax.broadcasted_iota(jnp.int32, (block, block), 0) + j * block
         seen = (key_at >= first) & (key_at <= last)
         bias[rows[j], :] = jnp.where(seen, 0.0, -1e30)
-        key_turned[:, rows[j]] = kv[j][:, :HEAD_SIZE].astype(jnp.float32).T.astype(jnp.bfloat16)
+        keys = kv[j][:, :HEAD_SIZE]
+        keys_ref[rows[j], :] = keys
+        values_ref[rows[j], :] = kv[j][:, HEAD_SIZE:]
+        key_turned[:, rows[j]] = keys.astype(jnp.float32).T.astype(jnp.bfloat16)
     terms = packed_ref[:, 2 * COLUMNS :].astype(jnp.float32).T
-    delta[...] = (
+    delta = (
         terms[:HEADS_EACH] + terms[HEADS_EACH : 2 * HEADS_EACH]
         + terms[2 * HEADS_EACH : 3 * HEADS_EACH]
     )
-    key_total[...] = jnp.zeros_like(key_total)
-    value_total[...] = jnp.zeros_like(value_total)
-
-    sub = 256
-    pieces = block * parts // sub
-    spans = [slice(i * sub, (i + 1) * sub) for i in range(pieces)]
-    group = 4
-    wide = group * block
-    def kvs(i, columns):
-        j, o = divmod(i * sub, block)
-        return kv[j][o : o + sub, columns]
-    for g in range(HEADS_EACH // group):
-        heads = range(g * group, (g + 1) * group)
-        query = jnp.concatenate([packed_ref[:, h * HEAD_SIZE : (h + 1) * HEAD_SIZE] for h in heads], axis=0)
-        grad = jnp.concatenate([packed_ref[:, COLUMNS + h * HEAD_SIZE : COLUMNS + (h + 1) * HEAD_SIZE] for h in heads], axis=0)
-        row_delta = jnp.concatenate([delta[h : h + 1, :] for h in heads], axis=1)
-        tops, sums = [], []
-        for i in range(pieces):
-            b = bias[spans[i], :]
-            if group > 1:
-                b = jnp.concatenate([b] * group, axis=1)
-            part = contract_last(kvs(i, slice(0, HEAD_SIZE)), query) * (SCALE * LOG2E) + b
-            top = jnp.max(part, axis=0, keepdims=True)
-            part = jnp.exp2(part - top)
-            scores[spans[i], :] = part.astype(scores.dtype)
-            tops.append(top)
-            sums.append(jnp.sum(part, axis=0, keepdims=True))
-        largest = tops[0]
-        for top in tops[1:]:
-            largest = jnp.maximum(largest, top)
-        factors = [jnp.exp2(top - largest) for top in tops]
-        total = factors[0] * sums[0]
-        for f, s in zip(factors[1:], sums[1:]):
-            total = total + f * s
-        inverse = 1.0 / total
-        query_grad = jnp.zeros((HEAD_SIZE, wide), jnp.float32)
-        for i in range(pieces):
-            probs = scores[spans[i], :].astype(jnp.float32) * (factors[i] * inverse)
-            value_total[spans[i], :] += jnp.dot(probs.astype(jnp.bfloat16), grad, preferred_element_type=jnp.float32)
-            grad_probs = contract_last(kvs(i, slice(HEAD_SIZE, 2 * HEAD_SIZE)), grad)
-            grad_scores = (probs * (grad_probs - row_delta)).astype(jnp.bfloat16)
-            key_total[spans[i], :] += jnp.dot(grad_scores, query, preferred_element_type=jnp.float32)
-            query_grad = query_grad + jnp.dot(key_turned[:, spans[i]], grad_scores, preferred_element_type=jnp.float32)
-        for n, h in enumerate(heads):
-            grad_query_ref[:, h * HEAD_SIZE : (h + 1) * HEAD_SIZE] = (query_grad[:, n * block : (n + 1) * block] * SCALE).T.astype(jnp.bfloat16)
+    row_delta = jnp.concatenate([delta[h : h + 1] for h in heads], axis=1)
+
+    def stacked(offset):
+        columns = [offset + h * HEAD_SIZE for h in heads]
+        return jnp.concatenate([packed_ref[:, c : c + HEAD_SIZE] for c in columns], axis=0)
+
+    query, grad = stacked(0), stacked(COLUMNS)
+    masks = jnp.concatenate([bias[...]] * HEADS_EACH, axis=1)
+    probs = contract_last(keys_ref[...], query) * (SCALE * LOG2E) + masks
+    probs = jnp.exp2(probs - jnp.max(probs, axis=0, keepdims=True))
+    probs = probs * (1.0 / jnp.sum(probs, axis=0, keepdims=True))
+    value_grad = jnp.dot(probs.astype(jnp.bfloat16), grad, preferred_element_type=jnp.float32)
+    grad_probs = contract_last(values_ref[...], grad)
+    grad_scores = (probs * (grad_probs - row_delta)).astype(jnp.bfloat16)
+    key_grad = jnp.dot(grad_scores, query, preferred_element_type=jnp.float32) * SCALE
+    query_grad = jnp.dot(key_turned[...], grad_scores, preferred_element_type=jnp.float32) * SCALE
+    for h in heads:
+        part = query_grad[:, h * block : (h + 1) * block]
+        grad_query_ref[:, h * HEAD_SIZE : (h + 1) * HEAD_SIZE] = part.T.astype(jnp.bfloat16)
     for j in range(parts):
-        outs[j][:, :HEAD_SIZE] = (key_total[rows[j], :] * SCALE).astype(outs[j].dtype)
-        outs[j][:, HEAD_SIZE:] = value_total[rows[j], :].astype(outs[j].dtype)
+        outs[j][:, :HEAD_SIZE] = key_grad[rows[j], :].astype(outs[j].dtype)
+        outs[j][:, HEAD_SIZE:] = value_grad[rows[j], :].astype(outs[j].dtype)
 
 
 def attend(packed, kv, first):
@@ -156,13 +146,11 @@
         out_specs=[VMEM] * (1 + len(kv)),
         scratch_shapes=[
             pltpu.VMEM((keys, block), jnp.float32),
+            pltpu.VMEM((keys, HEAD_SIZE), jnp.bfloat16),
+            pltpu.VMEM((keys, HEAD_SIZE), jnp.bfloat16),
             pltpu.VMEM((HEAD_SIZE, keys), jnp.bfloat16),
-            pltpu.VMEM((keys, 4 * block), jnp.float32),
-            pltpu.VMEM((HEADS_EACH, block), jnp.float32),
-            pltpu.VMEM((keys, HEAD_SIZE), jnp.float32),
-            pltpu.VMEM((keys, HEAD_SIZE), jnp.float32),
         ],
-        compiler_params=params(32),
+        compiler_params=params(50),
         name="attend",
     )(packed, *kv, first)
 

time: 83.6 us -> 81.3 us (0.972)
  local copies, waits for them, and re-layouts: 3.18 us -> 0.86 us
  Pallas kernels: 13.9 us -> 14.8 us
    pallas_call x0 -> x1, Pallas kernels: none -> 1.55 us  [pack_keys(): pl.pallas_call(pack_keys_kernel, out_shape=jax.ShapeDtypeStruct((KEY_VALU...]
    reshape x1 -> x0, local copies, waits for them, and re-layouts: 0.86 us -> none  [pack_keys(): x.reshape(rows, KEY_VALUE_HEADS, HEAD_SIZE)]
    unnamed x7 -> x5, local copies, waits for them, and re-layouts: 0.87 us -> 0.03 us
where the time goes in v3:
time: 81.3 us; the launch traced here: 80.6 us
  starting transfers between devices  42.6 us (52%)
  waiting for transfers between devices  20.6 us (25%)
  Pallas kernels  14.8 us (18%)
  other arithmetic  0.97 us (1%)
  local copies, waits for them, and re-layouts  0.86 us (1%)
    ppermute x8, starting transfers between devices, shift(): return lax.ppermute(value, ('ctx', 'head'), pairs)  25.8 us
    all_to_all x4, starting transfers between devices, exchange(): lax.all_to_all(value, 'head', split_axis=0, concat_axis=0, axis_index_gro...  16.9 us
    ppermute x8, waiting for transfers between devices, shift(): return lax.ppermute(value, ('ctx', 'head'), pairs)  13 us
    pallas_call x1, Pallas kernels, attend(): pl.pallas_call(attend_kernel, out_shape=[jax.ShapeDtypeStruct((block, COL...  8.5 us
    all_to_all x4, waiting for transfers between devices, exchange(): lax.all_to_all(value, 'head', split_axis=0, concat_axis=0, axis_index_gro...  7.56 us
    pallas_call x1, Pallas kernels, pack_queries(): pl.pallas_call(pack_queries_kernel, out_shape=jax.ShapeDtypeStruct((KEY_V...  2.83 us
    pallas_call x1, Pallas kernels, unpack_queries(): pl.pallas_call(unpack_queries_kernel, out_shape=jax.ShapeDtypeStruct((row...  1.87 us
  transfers between devices with their start and end apart: 12, of which 8 were waited for; matrix products, arithmetic and copies ran while one was open for 1% of the time, Pallas kernels for 6%

profile of v3, /device:TPU:248, one launch (start us, length us, event | category | flops | bytes accessed | tf_op | source)
XLA Modules:
  0.0 80.6 jit_solution(13080494746721509628)
XLA Ops:
  0.6 1.6 %pack_keys.1 = bf16[8,32,256]{2,1,0:T(8,128)(2,1)} custom-call(bf16[32,1024]{1,0:T(8,128)(2,1)} %key_ref.1, bf16[32,1024]{1,0:T(8,128)(2,1)} %value_ref.1), custom_call_target="tpu_custom_call" | custom-call | tf_op jit(solution)/shard_map/pack_keys/pallas_call | solution.py:40
  2.2 4.3 %all-to-all-start.1 = ((bf16[8,32,256]{2,1,0:T(8,128)(2,1)}), bf16[8,32,256]{2,1,0:T(8,128)(2,1)S(1)}, u32[]{:S(2)}, u32[]{:S(2)}) async-start(bf16[8,32,256]{2,1,0:T(8,128)(2,1)} %pack_keys.1), calls=%async_computation.1 | async-start | bytes 262144 | tf_op jit(solution)/shard_map/all_to_all | solution.py:199
  6.5 2.8 %pack_queries.1 = bf16[8,32,2176]{2,1,0:T(8,128)(2,1)} custom-call(bf16[32,8192]{1,0:T(8,128)(2,1)} %query_ref.1, bf16[32,8192]{1,0:T(8,128)(2,1)} %out_ref.1, bf16[32,8192]{1,0:T(8,128)(2,1)} %grad_ref.1), custom_call_target="tpu_custom_call" | custom-call | tf_op jit(solution)/shard_map/pack_queries/pallas_call | solution.py:75
  9.3 3.3 %all-to-all-done.1 = bf16[8,32,256]{2,1,0:T(8,128)(2,1)S(1)} async-done(((bf16[8,32,256]{2,1,0:T(8,128)(2,1)}), bf16[8,32,256]{2,1,0:T(8,128)(2,1)S(1)}, u32[]{:S(2)}, u32[]{:S(2)}) %all-to-all-start.1) | async-done | bytes 131104 | tf_op jit(solution)/shard_map/all_to_all | solution.py:199
  12.6 3.6 %all-to-all-start = ((bf16[8,32,2176]{2,1,0:T(8,128)(2,1)}), bf16[8,32,2176]{2,1,0:T(8,128)(2,1)S(1)}, u32[]{:S(2)}, u32[]{:S(2)}) async-start(bf16[8,32,2176]{2,1,0:T(8,128)(2,1)} %pack_queries.1), calls=%async_computation | async-start | bytes 2228224 | tf_op jit(solution)/shard_map/all_to_all | solution.py:199
  16.2 0.1 pad_dynamic-slice_fusion.1
  16.3 4.7 %collective-permute-start.3 = (bf16[256,256]{1,0:T(8,128)(2,1)S(1)}, bf16[256,256]{1,0:T(8,128)(2,1)S(1)}, u32[]{:S(2)}, u32[]{:S(2)}) collective-permute-start(bf16[256,256]{1,0:T(8,128)(2,1)S(1)} %bitcast.15), channel_id=1, source_target_pairs={{0,8},{1,9},{2,10},{3,11},{4,12},{5,13},{6,14},{7,15},{8,16},{9,17... | collective-permute-start | bytes 393224 | tf_op jit(solution)/shard_map/ppermute | solution.py:211
  21.0 4.5 %collective-permute-start.2 = (bf16[256,256]{1,0:T(8,128)(2,1)S(1)}, bf16[256,256]{1,0:T(8,128)(2,1)S(1)}, u32[]{:S(2)}, u32[]{:S(2)}) collective-permute-start(bf16[256,256]{1,0:T(8,128)(2,1)S(1)} %bitcast.16), channel_id=1, source_target_pairs={{0,16},{1,17},{2,18},{3,19},{4,20},{5,21},{6,22},{7,23},{8,24},{9,... | collective-permute-start | bytes 393224 | tf_op jit(solution)/shard_map/ppermute | solution.py:211
  25.5 2.2 %collective-permute-start.1 = (bf16[256,256]{1,0:T(8,128)(2,1)S(1)}, bf16[256,256]{1,0:T(8,128)(2,1)S(1)}, u32[]{:S(2)}, u32[]{:S(2)}) collective-permute-start(bf16[256,256]{1,0:T(8,128)(2,1)S(1)} %bitcast.17), channel_id=1, source_target_pairs={{0,24},{1,25},{2,26},{3,27},{4,28},{5,29},{6,30},{7,31},{8,32},{9,... | collective-permute-start | bytes 393224 | tf_op jit(solution)/shard_map/ppermute | solution.py:211
  27.7 2.9 %collective-permute-start = (bf16[256,256]{1,0:T(8,128)(2,1)S(1)}, bf16[256,256]{1,0:T(8,128)(2,1)S(1)}, u32[]{:S(2)}, u32[]{:S(2)}) collective-permute-start(bf16[256,256]{1,0:T(8,128)(2,1)S(1)} %bitcast.18), channel_id=1, source_target_pairs={{0,32},{1,33},{2,34},{3,35},{4,36},{5,37},{6,38},{7,39},{8,40},{9,... | collective-permute-start | bytes 393224 | tf_op jit(solution)/shard_map/ppermute | solution.py:211
  30.7 0.1 pad_dynamic-slice_fusion
  30.7 0.2 convert_reduce_fusion
  31.0 0.0 collective-permute-done.3.kv3
  31.0 1.8 %collective-permute-done.2.kv2 = bf16[256,256]{1,0:T(8,128)(2,1)S(1)} collective-permute-done((bf16[256,256]{1,0:T(8,128)(2,1)S(1)}, bf16[256,256]{1,0:T(8,128)(2,1)S(1)}, u32[]{:S(2)}, u32[]{:S(2)}) %collective-permute-start.2) | collective-permute-done | bytes 131104 | tf_op jit(solution)/shard_map/ppermute | solution.py:211
  32.8 1.3 %collective-permute-done.1.kv1 = bf16[256,256]{1,0:T(8,128)(2,1)S(1)} collective-permute-done((bf16[256,256]{1,0:T(8,128)(2,1)S(1)}, bf16[256,256]{1,0:T(8,128)(2,1)S(1)}, u32[]{:S(2)}, u32[]{:S(2)}) %collective-permute-start.1) | collective-permute-done | bytes 131104 | tf_op jit(solution)/shard_map/ppermute | solution.py:211
  34.1 0.5 collective-permute-done.kv0
  34.7 0.0 all-to-all-done
  34.7 8.5 %attend.1 = (bf16[256,1024]{1,0:T(8,128)(2,1)}, bf16[256,256]{1,0:T(8,128)(2,1)S(1)}, bf16[256,256]{1,0:T(8,128)(2,1)S(1)}, bf16[256,256]{1,0:T(8,128)(2,1)S(1)}...) custom-call(bf16[256,2176]{1,0:T(8,128)(2,1)S(1)} %bitcast.14, bf16[256,256]{1,0:T(8,128)(2,1)S(1)} %collective-permute-done.kv0, ...), custom_call_target="tpu_custom_call" | custom-call | tf_op jit(solution)/shard_map/attend/pallas_call | solution.py:140
  43.2 4.6 %all-to-all-start.2 = ((bf16[8,32,1024]{2,1,0:T(8,128)(2,1)}), bf16[8,32,1024]{2,1,0:T(8,128)(2,1)S(1)}, u32[]{:S(2)}, u32[]{:S(2)}) async-start(bf16[8,32,1024]{2,1,0:T(8,128)(2,1)} %bitcast.3), calls=%async_computation.2 | async-start | bytes 1048576 | tf_op jit(solution)/shard_map/all_to_all | solution.py:199
  47.8 2.9 %collective-permute-start.4 = (bf16[256,256]{1,0:T(8,128)(2,1)S(1)}, bf16[256,256]{1,0:T(8,128)(2,1)S(1)}, u32[]{:S(2)}, u32[]{:S(2)}) collective-permute-start(bf16[256,256]{1,0:T(8,128)(2,1)S(1)} %get-tuple-element.12), channel_id=1, source_target_pairs={{32,0},{33,1},{34,2},{35,3},{36,4},{37,5},{38,6},{39,7},{40,8},{41... | collective-permute-start | bytes 393224 | tf_op jit(solution)/shard_map/ppermute | solution.py:211
  50.7 3.9 %collective-permute-start.5 = (bf16[256,256]{1,0:T(8,128)(2,1)S(1)}, bf16[256,256]{1,0:T(8,128)(2,1)S(1)}, u32[]{:S(2)}, u32[]{:S(2)}) collective-permute-start(bf16[256,256]{1,0:T(8,128)(2,1)S(1)} %get-tuple-element.13), channel_id=1, source_target_pairs={{24,0},{25,1},{26,2},{27,3},{28,4},{29,5},{30,6},{31,7},{32,8},{33... | collective-permute-start | bytes 393224 | tf_op jit(solution)/shard_map/ppermute | solution.py:211
  54.5 2.5 %collective-permute-start.6 = (bf16[256,256]{1,0:T(8,128)(2,1)S(1)}, bf16[256,256]{1,0:T(8,128)(2,1)S(1)}, u32[]{:S(2)}, u32[]{:S(2)}) collective-permute-start(bf16[256,256]{1,0:T(8,128)(2,1)S(1)} %get-tuple-element.14), channel_id=1, source_target_pairs={{16,0},{17,1},{18,2},{19,3},{20,4},{21,5},{22,6},{23,7},{24,8},{25... | collective-permute-start | bytes 393224 | tf_op jit(solution)/shard_map/ppermute | solution.py:211
  57.1 2.2 %collective-permute-start.7 = (bf16[256,256]{1,0:T(8,128)(2,1)S(1)}, bf16[256,256]{1,0:T(8,128)(2,1)S(1)}, u32[]{:S(2)}, u32[]{:S(2)}) collective-permute-start(bf16[256,256]{1,0:T(8,128)(2,1)S(1)} %get-tuple-element.15), channel_id=1, source_target_pairs={{8,0},{9,1},{10,2},{11,3},{12,4},{13,5},{14,6},{15,7},{16,8},{17,9... | collective-permute-start | bytes 393224 | tf_op jit(solution)/shard_map/ppermute | solution.py:211
  59.2 0.0 collective-permute-done.4
  59.2 1.2 %collective-permute-done.5 = bf16[256,256]{1,0:T(8,128)(2,1)S(1)} collective-permute-done((bf16[256,256]{1,0:T(8,128)(2,1)S(1)}, bf16[256,256]{1,0:T(8,128)(2,1)S(1)}, u32[]{:S(2)}, u32[]{:S(2)}) %collective-permute-start.5) | collective-permute-done | bytes 131104 | tf_op jit(solution)/shard_map/ppermute | solution.py:211
  60.4 6.3 %collective-permute-done.6 = bf16[256,256]{1,0:T(8,128)(2,1)S(1)} collective-permute-done((bf16[256,256]{1,0:T(8,128)(2,1)S(1)}, bf16[256,256]{1,0:T(8,128)(2,1)S(1)}, u32[]{:S(2)}, u32[]{:S(2)}) %collective-permute-start.6) | collective-permute-done | bytes 131104 | tf_op jit(solution)/shard_map/ppermute | solution.py:211
  66.7 1.9 %collective-permute-done.7 = bf16[256,256]{1,0:T(8,128)(2,1)S(1)} collective-permute-done((bf16[256,256]{1,0:T(8,128)(2,1)S(1)}, bf16[256,256]{1,0:T(8,128)(2,1)S(1)}, u32[]{:S(2)}, u32[]{:S(2)}) %collective-permute-start.7) | collective-permute-done | bytes 131104 | tf_op jit(solution)/shard_map/ppermute | solution.py:211
  68.6 0.7 add_convert_fusion
  69.3 4.4 %all-to-all-start.3 = ((bf16[8,32,256]{2,1,0:T(8,128)(2,1)}), bf16[8,32,256]{2,1,0:T(8,128)(2,1)S(1)}, u32[]{:S(2)}, u32[]{:S(2)}) async-start(bf16[8,32,256]{2,1,0:T(8,128)(2,1)} %bitcast.4), calls=%async_computation.3 | async-start | bytes 262144 | tf_op jit(solution)/shard_map/all_to_all | solution.py:199
  73.8 1.9 %unpack_queries.1 = bf16[32,8192]{1,0:T(8,128)(2,1)} custom-call(bf16[8,32,1024]{2,1,0:T(8,128)(2,1)} %copy-done), custom_call_target="tpu_custom_call" | custom-call | tf_op jit(solution)/shard_map/unpack_queries/pallas_call | solution.py:171
  75.6 4.3 %all-to-all-done.3 = bf16[8,32,256]{2,1,0:T(8,128)(2,1)S(1)} async-done(((bf16[8,32,256]{2,1,0:T(8,128)(2,1)}), bf16[8,32,256]{2,1,0:T(8,128)(2,1)S(1)}, u32[]{:S(2)}, u32[]{:S(2)}) %all-to-all-start.3) | async-done | bytes 131104 | tf_op jit(solution)/shard_map/all_to_all | solution.py:199
  79.9 0.7 copy_bitcast_fusion
  (6 shorter events, 0.0 us)
Async XLA Ops:
  2.2 10.4 %all-to-all-start.1 = ((bf16[8,32,256]{2,1,0:T(8,128)(2,1)}), bf16[8,32,256]{2,1,0:T(8,128)(2,1)S(1)}, u32[]{:S(2)}, u32[]{:S(2)}) async-start(bf16[8,32,256]{2,1,0:T(8,128)(2,1)} %pack_keys.1), calls=%async_computation.1 | async-start | bytes 262144 | tf_op jit(solution)/shard_map/all_to_all | solution.py:199
  9.3 6.9 %copy-start.1 = (s32[16384]{0:T(1024)S(1)}, s32[16384]{0:T(1024)}, u32[]{:S(2)}) copy-start(s32[16384]{0:T(1024)} %param.11) | copy-start | bytes 196612
  12.6 22.1 %all-to-all-start = ((bf16[8,32,2176]{2,1,0:T(8,128)(2,1)}), bf16[8,32,2176]{2,1,0:T(8,128)(2,1)S(1)}, u32[]{:S(2)}, u32[]{:S(2)}) async-start(bf16[8,32,2176]{2,1,0:T(8,128)(2,1)} %pack_queries.1), calls=%async_computation | async-start | bytes 2228224 | tf_op jit(solution)/shard_map/all_to_all | solution.py:199
  16.3 14.7 %collective-permute-start.3 = (bf16[256,256]{1,0:T(8,128)(2,1)S(1)}, bf16[256,256]{1,0:T(8,128)(2,1)S(1)}, u32[]{:S(2)}, u32[]{:S(2)}) collective-permute-start(bf16[256,256]{1,0:T(8,128)(2,1)S(1)} %bitcast.15), channel_id=1, source_target_pairs={{0,8},{1,9},{2,10},{3,11},{4,12},{5,13},{6,14},{7,15},{8,16},{9,17... | collective-permute-start | bytes 393224 | tf_op jit(solution)/shard_map/ppermute | solution.py:211
  21.0 11.8 %collective-permute-start.2 = (bf16[256,256]{1,0:T(8,128)(2,1)S(1)}, bf16[256,256]{1,0:T(8,128)(2,1)S(1)}, u32[]{:S(2)}, u32[]{:S(2)}) collective-permute-start(bf16[256,256]{1,0:T(8,128)(2,1)S(1)} %bitcast.16), channel_id=1, source_target_pairs={{0,16},{1,17},{2,18},{3,19},{4,20},{5,21},{6,22},{7,23},{8,24},{9,... | collective-permute-start | bytes 393224 | tf_op jit(solution)/shard_map/ppermute | solution.py:211
  25.5 8.6 %collective-permute-start.1 = (bf16[256,256]{1,0:T(8,128)(2,1)S(1)}, bf16[256,256]{1,0:T(8,128)(2,1)S(1)}, u32[]{:S(2)}, u32[]{:S(2)}) collective-permute-start(bf16[256,256]{1,0:T(8,128)(2,1)S(1)} %bitcast.17), channel_id=1, source_target_pairs={{0,24},{1,25},{2,26},{3,27},{4,28},{5,29},{6,30},{7,31},{8,32},{9,... | collective-permute-start | bytes 393224 | tf_op jit(solution)/shard_map/ppermute | solution.py:211
  27.7 7.0 %collective-permute-start = (bf16[256,256]{1,0:T(8,128)(2,1)S(1)}, bf16[256,256]{1,0:T(8,128)(2,1)S(1)}, u32[]{:S(2)}, u32[]{:S(2)}) collective-permute-start(bf16[256,256]{1,0:T(8,128)(2,1)S(1)} %bitcast.18), channel_id=1, source_target_pairs={{0,32},{1,33},{2,34},{3,35},{4,36},{5,37},{6,38},{7,39},{8,40},{9,... | collective-permute-start | bytes 393224 | tf_op jit(solution)/shard_map/ppermute | solution.py:211
  43.2 26.1 %all-to-all-start.2 = ((bf16[8,32,1024]{2,1,0:T(8,128)(2,1)}), bf16[8,32,1024]{2,1,0:T(8,128)(2,1)S(1)}, u32[]{:S(2)}, u32[]{:S(2)}) async-start(bf16[8,32,1024]{2,1,0:T(8,128)(2,1)} %bitcast.3), calls=%async_computation.2 | async-start | bytes 1048576 | tf_op jit(solution)/shard_map/all_to_all | solution.py:199
  47.8 11.5 %collective-permute-start.4 = (bf16[256,256]{1,0:T(8,128)(2,1)S(1)}, bf16[256,256]{1,0:T(8,128)(2,1)S(1)}, u32[]{:S(2)}, u32[]{:S(2)}) collective-permute-start(bf16[256,256]{1,0:T(8,128)(2,1)S(1)} %get-tuple-element.12), channel_id=1, source_target_pairs={{32,0},{33,1},{34,2},{35,3},{36,4},{37,5},{38,6},{39,7},{40,8},{41... | collective-permute-start | bytes 393224 | tf_op jit(solution)/shard_map/ppermute | solution.py:211
  50.7 9.7 %collective-permute-start.5 = (bf16[256,256]{1,0:T(8,128)(2,1)S(1)}, bf16[256,256]{1,0:T(8,128)(2,1)S(1)}, u32[]{:S(2)}, u32[]{:S(2)}) collective-permute-start(bf16[256,256]{1,0:T(8,128)(2,1)S(1)} %get-tuple-element.13), channel_id=1, source_target_pairs={{24,0},{25,1},{26,2},{27,3},{28,4},{29,5},{30,6},{31,7},{32,8},{33... | collective-permute-start | bytes 393224 | tf_op jit(solution)/shard_map/ppermute | solution.py:211
  54.5 12.2 %collective-permute-start.6 = (bf16[256,256]{1,0:T(8,128)(2,1)S(1)}, bf16[256,256]{1,0:T(8,128)(2,1)S(1)}, u32[]{:S(2)}, u32[]{:S(2)}) collective-permute-start(bf16[256,256]{1,0:T(8,128)(2,1)S(1)} %get-tuple-element.14), channel_id=1, source_target_pairs={{16,0},{17,1},{18,2},{19,3},{20,4},{21,5},{22,6},{23,7},{24,8},{25... | collective-permute-start | bytes 393224 | tf_op jit(solution)/shard_map/ppermute | solution.py:211
  57.1 11.5 %collective-permute-start.7 = (bf16[256,256]{1,0:T(8,128)(2,1)S(1)}, bf16[256,256]{1,0:T(8,128)(2,1)S(1)}, u32[]{:S(2)}, u32[]{:S(2)}) collective-permute-start(bf16[256,256]{1,0:T(8,128)(2,1)S(1)} %get-tuple-element.15), channel_id=1, source_target_pairs={{8,0},{9,1},{10,2},{11,3},{12,4},{13,5},{14,6},{15,7},{16,8},{17,9... | collective-permute-start | bytes 393224 | tf_op jit(solution)/shard_map/ppermute | solution.py:211
  69.3 4.5 %copy-start = (bf16[8,32,1024]{2,1,0:T(8,128)(2,1)}, bf16[8,32,1024]{2,1,0:T(8,128)(2,1)S(1)}, u32[]{:S(2)}) copy-start(bf16[8,32,1024]{2,1,0:T(8,128)(2,1)S(1)} %all-to-all-done.2.in_ref) | copy-start | bytes 1572868
  69.3 10.6 %all-to-all-start.3 = ((bf16[8,32,256]{2,1,0:T(8,128)(2,1)}), bf16[8,32,256]{2,1,0:T(8,128)(2,1)S(1)}, u32[]{:S(2)}, u32[]{:S(2)}) async-start(bf16[8,32,256]{2,1,0:T(8,128)(2,1)} %bitcast.4), calls=%async_computation.3 | async-start | bytes 262144 | tf_op jit(solution)/shard_map/all_to_all | solution.py:199

commit v4 on v3

--- a/solution.py
+++ b/solution.py
@@ -86,7 +86,7 @@
 def attend_kernel(
     packed_ref, kv0, kv1, kv2, kv3, kv4, first_ref,
     grad_query_ref, out0, out1, out2, out3, out4,
-    bias, keys_ref, values_ref, key_turned,
+    bias, keys_ref, values_ref, key_turned, key_total, value_total,
 ):
     kv = (kv0, kv1, kv2, kv3, kv4)
     outs = (out0, out1, out2, out3, out4)
@@ -109,28 +109,59 @@
         terms[:HEADS_EACH] + terms[HEADS_EACH : 2 * HEADS_EACH]
         + terms[2 * HEADS_EACH : 3 * HEADS_EACH]
     )
-    row_delta = jnp.concatenate([delta[h : h + 1] for h in heads], axis=1)
-
-    def stacked(offset):
-        columns = [offset + h * HEAD_SIZE for h in heads]
-        return jnp.concatenate([packed_ref[:, c : c + HEAD_SIZE] for c in columns], axis=0)
-
-    query, grad = stacked(0), stacked(COLUMNS)
-    masks = jnp.concatenate([bias[...]] * HEADS_EACH, axis=1)
-    probs = contract_last(keys_ref[...], query) * (SCALE * LOG2E) + masks
-    probs = jnp.exp2(probs - jnp.max(probs, axis=0, keepdims=True))
-    probs = probs * (1.0 / jnp.sum(probs, axis=0, keepdims=True))
-    value_grad = jnp.dot(probs.astype(jnp.bfloat16), grad, preferred_element_type=jnp.float32)
-    grad_probs = contract_last(values_ref[...], grad)
-    grad_scores = (probs * (grad_probs - row_delta)).astype(jnp.bfloat16)
-    key_grad = jnp.dot(grad_scores, query, preferred_element_type=jnp.float32) * SCALE
-    query_grad = jnp.dot(key_turned[...], grad_scores, preferred_element_type=jnp.float32) * SCALE
-    for h in heads:
-        part = query_grad[:, h * block : (h + 1) * block]
-        grad_query_ref[:, h * HEAD_SIZE : (h + 1) * HEAD_SIZE] = part.T.astype(jnp.bfloat16)
+    step = block // 2
+    reach = (parts - 1) * block + step
+
+    def weigh(part):
+        token = slice(part * step, (part + 1) * step)
+        near = slice(part * step, part * step + reach)
+
+        def stacked(offset):
+            columns = [offset + h * HEAD_SIZE for h in heads]
+            return jnp.concatenate([packed_ref[token, c : c + HEAD_SIZE] for c in columns], axis=0)
+
+        query, grad = stacked(0), stacked(COLUMNS)
+        masks = jnp.concatenate([bias[near, token]] * HEADS_EACH, axis=1)
+        raw = contract_last(keys_ref[near, :], query) * (SCALE * LOG2E) + masks
+        return query, grad, raw, jnp.max(raw, axis=0, keepdims=True)
+
+    def normalize(part, query, grad, raw, largest):
+        near = slice(part * step, part * step + reach)
+        weights = jnp.exp2(raw - largest)
+        inverse = 1.0 / jnp.sum(weights, axis=0, keepdims=True)
+        return query, grad, weights, inverse, contract_last(values_ref[near, :], grad)
+
+    def finish(part, query, grad, weights, inverse, grad_probs):
+        token = slice(part * step, (part + 1) * step)
+        near = slice(part * step, part * step + reach)
+        row_delta = jnp.concatenate([delta[h : h + 1, token] for h in heads], axis=1)
+        probs = weights * inverse
+        grad_scores = (probs * (grad_probs - row_delta)).astype(jnp.bfloat16)
+        value_grad = jnp.dot(probs.astype(jnp.bfloat16), grad, preferred_element_type=jnp.float32)
+        key_grad = jnp.dot(grad_scores, query, preferred_element_type=jnp.float32)
+        query_grad = (
+            jnp.dot(key_turned[:, near], grad_scores, preferred_element_type=jnp.float32) * SCALE
+        )
+        for h in heads:
+            turned = query_grad[:, h * step : (h + 1) * step].T.astype(jnp.bfloat16)
+            grad_query_ref[token, h * HEAD_SIZE : (h + 1) * HEAD_SIZE] = turned
+        if part == 0:
+            key_total[near, :] = key_grad
+            value_total[near, :] = value_grad
+        else:
+            both, new = slice(near.start, reach), slice(reach, near.stop)
+            key_total[both, :] += key_grad[: reach - step]
+            value_total[both, :] += value_grad[: reach - step]
+            key_total[new, :] = key_grad[reach - step :]
+            value_total[new, :] = value_grad[reach - step :]
+
+    weighed = [weigh(part) for part in range(2)]
+    normal = [normalize(part, *weighed[part]) for part in range(2)]
+    for part in range(2):
+        finish(part, *normal[part])
     for j in range(parts):
-        outs[j][:, :HEAD_SIZE] = key_grad[rows[j], :].astype(outs[j].dtype)
-        outs[j][:, HEAD_SIZE:] = value_grad[rows[j], :].astype(outs[j].dtype)
+        outs[j][:, :HEAD_SIZE] = (key_total[rows[j], :] * SCALE).astype(outs[j].dtype)
+        outs[j][:, HEAD_SIZE:] = value_total[rows[j], :].astype(outs[j].dtype)
 
 
 def attend(packed, kv, first):
@@ -149,6 +180,8 @@
             pltpu.VMEM((keys, HEAD_SIZE), jnp.bfloat16),
             pltpu.VMEM((keys, HEAD_SIZE), jnp.bfloat16),
             pltpu.VMEM((HEAD_SIZE, keys), jnp.bfloat16),
+            pltpu.VMEM((keys, HEAD_SIZE), jnp.float32),
+            pltpu.VMEM((keys, HEAD_SIZE), jnp.float32),
         ],
         compiler_params=params(50),
         name="attend",

time: 81.3 us -> 80.6 us (level)
  no operation moved by 1% of the time
where the time goes in v4:
time: 80.6 us; the launch traced here: 79.8 us
  starting transfers between devices  42.6 us (53%)
  waiting for transfers between devices  20.6 us (26%)
  Pallas kernels  14 us (17%)
  other arithmetic  0.97 us (1%)
  local copies, waits for them, and re-layouts  0.86 us (1%)
    ppermute x8, starting transfers between devices, shift(): return lax.ppermute(value, ('ctx', 'head'), pairs)  25.8 us
    all_to_all x4, starting transfers between devices, exchange(): lax.all_to_all(value, 'head', split_axis=0, concat_axis=0, axis_index_gro...  16.9 us
    ppermute x8, waiting for transfers between devices, shift(): return lax.ppermute(value, ('ctx', 'head'), pairs)  13 us
    pallas_call x1, Pallas kernels, attend(): pl.pallas_call(attend_kernel, out_shape=[jax.ShapeDtypeStruct((block, COL...  7.73 us
    all_to_all x4, waiting for transfers between devices, exchange(): lax.all_to_all(value, 'head', split_axis=0, concat_axis=0, axis_index_gro...  7.56 us
    pallas_call x1, Pallas kernels, pack_queries(): pl.pallas_call(pack_queries_kernel, out_shape=jax.ShapeDtypeStruct((KEY_V...  2.83 us
    pallas_call x1, Pallas kernels, unpack_queries(): pl.pallas_call(unpack_queries_kernel, out_shape=jax.ShapeDtypeStruct((row...  1.87 us
  transfers between devices with their start and end apart: 12, of which 8 were waited for; matrix products, arithmetic and copies ran while one was open for 1% of the time, Pallas kernels for 6%

profile of v4, /device:TPU:248, one launch (start us, length us, event | category | flops | bytes accessed | tf_op | source)
XLA Modules:
  0.0 79.8 jit_solution(13824528075885583071)
XLA Ops:
  0.6 1.6 %pack_keys.1 = bf16[8,32,256]{2,1,0:T(8,128)(2,1)} custom-call(bf16[32,1024]{1,0:T(8,128)(2,1)} %key_ref.1, bf16[32,1024]{1,0:T(8,128)(2,1)} %value_ref.1), custom_call_target="tpu_custom_call" | custom-call | tf_op jit(solution)/shard_map/pack_keys/pallas_call | solution.py:40
  2.2 4.3 %all-to-all-start.1 = ((bf16[8,32,256]{2,1,0:T(8,128)(2,1)}), bf16[8,32,256]{2,1,0:T(8,128)(2,1)S(1)}, u32[]{:S(2)}, u32[]{:S(2)}) async-start(bf16[8,32,256]{2,1,0:T(8,128)(2,1)} %pack_keys.1), calls=%async_computation.1 | async-start | bytes 262144 | tf_op jit(solution)/shard_map/all_to_all | solution.py:232
  6.5 2.8 %pack_queries.1 = bf16[8,32,2176]{2,1,0:T(8,128)(2,1)} custom-call(bf16[32,8192]{1,0:T(8,128)(2,1)} %query_ref.1, bf16[32,8192]{1,0:T(8,128)(2,1)} %out_ref.1, bf16[32,8192]{1,0:T(8,128)(2,1)} %grad_ref.1), custom_call_target="tpu_custom_call" | custom-call | tf_op jit(solution)/shard_map/pack_queries/pallas_call | solution.py:75
  9.3 3.3 %all-to-all-done.1 = bf16[8,32,256]{2,1,0:T(8,128)(2,1)S(1)} async-done(((bf16[8,32,256]{2,1,0:T(8,128)(2,1)}), bf16[8,32,256]{2,1,0:T(8,128)(2,1)S(1)}, u32[]{:S(2)}, u32[]{:S(2)}) %all-to-all-start.1) | async-done | bytes 131104 | tf_op jit(solution)/shard_map/all_to_all | solution.py:232
  12.6 3.6 %all-to-all-start = ((bf16[8,32,2176]{2,1,0:T(8,128)(2,1)}), bf16[8,32,2176]{2,1,0:T(8,128)(2,1)S(1)}, u32[]{:S(2)}, u32[]{:S(2)}) async-start(bf16[8,32,2176]{2,1,0:T(8,128)(2,1)} %pack_queries.1), calls=%async_computation | async-start | bytes 2228224 | tf_op jit(solution)/shard_map/all_to_all | solution.py:232
  16.2 0.1 pad_dynamic-slice_fusion.1
  16.3 4.7 %collective-permute-start.3 = (bf16[256,256]{1,0:T(8,128)(2,1)S(1)}, bf16[256,256]{1,0:T(8,128)(2,1)S(1)}, u32[]{:S(2)}, u32[]{:S(2)}) collective-permute-start(bf16[256,256]{1,0:T(8,128)(2,1)S(1)} %bitcast.15), channel_id=1, source_target_pairs={{0,8},{1,9},{2,10},{3,11},{4,12},{5,13},{6,14},{7,15},{8,16},{9,17... | collective-permute-start | bytes 393224 | tf_op jit(solution)/shard_map/ppermute | solution.py:244
  21.0 4.5 %collective-permute-start.2 = (bf16[256,256]{1,0:T(8,128)(2,1)S(1)}, bf16[256,256]{1,0:T(8,128)(2,1)S(1)}, u32[]{:S(2)}, u32[]{:S(2)}) collective-permute-start(bf16[256,256]{1,0:T(8,128)(2,1)S(1)} %bitcast.16), channel_id=1, source_target_pairs={{0,16},{1,17},{2,18},{3,19},{4,20},{5,21},{6,22},{7,23},{8,24},{9,... | collective-permute-start | bytes 393224 | tf_op jit(solution)/shard_map/ppermute | solution.py:244
  25.5 2.2 %collective-permute-start.1 = (bf16[256,256]{1,0:T(8,128)(2,1)S(1)}, bf16[256,256]{1,0:T(8,128)(2,1)S(1)}, u32[]{:S(2)}, u32[]{:S(2)}) collective-permute-start(bf16[256,256]{1,0:T(8,128)(2,1)S(1)} %bitcast.17), channel_id=1, source_target_pairs={{0,24},{1,25},{2,26},{3,27},{4,28},{5,29},{6,30},{7,31},{8,32},{9,... | collective-permute-start | bytes 393224 | tf_op jit(solution)/shard_map/ppermute | solution.py:244
  27.7 2.9 %collective-permute-start = (bf16[256,256]{1,0:T(8,128)(2,1)S(1)}, bf16[256,256]{1,0:T(8,128)(2,1)S(1)}, u32[]{:S(2)}, u32[]{:S(2)}) collective-permute-start(bf16[256,256]{1,0:T(8,128)(2,1)S(1)} %bitcast.18), channel_id=1, source_target_pairs={{0,32},{1,33},{2,34},{3,35},{4,36},{5,37},{6,38},{7,39},{8,40},{9,... | collective-permute-start | bytes 393224 | tf_op jit(solution)/shard_map/ppermute | solution.py:244
  30.7 0.1 pad_dynamic-slice_fusion
  30.7 0.2 convert_reduce_fusion
  31.0 0.0 collective-permute-done.3.kv3
  31.0 1.8 %collective-permute-done.2.kv2 = bf16[256,256]{1,0:T(8,128)(2,1)S(1)} collective-permute-done((bf16[256,256]{1,0:T(8,128)(2,1)S(1)}, bf16[256,256]{1,0:T(8,128)(2,1)S(1)}, u32[]{:S(2)}, u32[]{:S(2)}) %collective-permute-start.2) | collective-permute-done | bytes 131104 | tf_op jit(solution)/shard_map/ppermute | solution.py:244
  32.8 1.3 %collective-permute-done.1.kv1 = bf16[256,256]{1,0:T(8,128)(2,1)S(1)} collective-permute-done((bf16[256,256]{1,0:T(8,128)(2,1)S(1)}, bf16[256,256]{1,0:T(8,128)(2,1)S(1)}, u32[]{:S(2)}, u32[]{:S(2)}) %collective-permute-start.1) | collective-permute-done | bytes 131104 | tf_op jit(solution)/shard_map/ppermute | solution.py:244
  34.1 0.5 collective-permute-done.kv0
  34.7 0.0 all-to-all-done
  34.7 7.7 %attend.1 = (bf16[256,1024]{1,0:T(8,128)(2,1)}, bf16[256,256]{1,0:T(8,128)(2,1)S(1)}, bf16[256,256]{1,0:T(8,128)(2,1)S(1)}, bf16[256,256]{1,0:T(8,128)(2,1)S(1)}...) custom-call(bf16[256,2176]{1,0:T(8,128)(2,1)S(1)} %bitcast.14, bf16[256,256]{1,0:T(8,128)(2,1)S(1)} %collective-permute-done.kv0, ...), custom_call_target="tpu_custom_call" | custom-call | tf_op jit(solution)/shard_map/attend/pallas_call | solution.py:171
  42.4 4.6 %all-to-all-start.2 = ((bf16[8,32,1024]{2,1,0:T(8,128)(2,1)}), bf16[8,32,1024]{2,1,0:T(8,128)(2,1)S(1)}, u32[]{:S(2)}, u32[]{:S(2)}) async-start(bf16[8,32,1024]{2,1,0:T(8,128)(2,1)} %bitcast.3), calls=%async_computation.2 | async-start | bytes 1048576 | tf_op jit(solution)/shard_map/all_to_all | solution.py:232
  47.0 2.9 %collective-permute-start.4 = (bf16[256,256]{1,0:T(8,128)(2,1)S(1)}, bf16[256,256]{1,0:T(8,128)(2,1)S(1)}, u32[]{:S(2)}, u32[]{:S(2)}) collective-permute-start(bf16[256,256]{1,0:T(8,128)(2,1)S(1)} %get-tuple-element.12), channel_id=1, source_target_pairs={{32,0},{33,1},{34,2},{35,3},{36,4},{37,5},{38,6},{39,7},{40,8},{41... | collective-permute-start | bytes 393224 | tf_op jit(solution)/shard_map/ppermute | solution.py:244
  49.9 3.9 %collective-permute-start.5 = (bf16[256,256]{1,0:T(8,128)(2,1)S(1)}, bf16[256,256]{1,0:T(8,128)(2,1)S(1)}, u32[]{:S(2)}, u32[]{:S(2)}) collective-permute-start(bf16[256,256]{1,0:T(8,128)(2,1)S(1)} %get-tuple-element.13), channel_id=1, source_target_pairs={{24,0},{25,1},{26,2},{27,3},{28,4},{29,5},{30,6},{31,7},{32,8},{33... | collective-permute-start | bytes 393224 | tf_op jit(solution)/shard_map/ppermute | solution.py:244
  53.8 2.5 %collective-permute-start.6 = (bf16[256,256]{1,0:T(8,128)(2,1)S(1)}, bf16[256,256]{1,0:T(8,128)(2,1)S(1)}, u32[]{:S(2)}, u32[]{:S(2)}) collective-permute-start(bf16[256,256]{1,0:T(8,128)(2,1)S(1)} %get-tuple-element.14), channel_id=1, source_target_pairs={{16,0},{17,1},{18,2},{19,3},{20,4},{21,5},{22,6},{23,7},{24,8},{25... | collective-permute-start | bytes 393224 | tf_op jit(solution)/shard_map/ppermute | solution.py:244
  56.3 2.2 %collective-permute-start.7 = (bf16[256,256]{1,0:T(8,128)(2,1)S(1)}, bf16[256,256]{1,0:T(8,128)(2,1)S(1)}, u32[]{:S(2)}, u32[]{:S(2)}) collective-permute-start(bf16[256,256]{1,0:T(8,128)(2,1)S(1)} %get-tuple-element.15), channel_id=1, source_target_pairs={{8,0},{9,1},{10,2},{11,3},{12,4},{13,5},{14,6},{15,7},{16,8},{17,9... | collective-permute-start | bytes 393224 | tf_op jit(solution)/shard_map/ppermute | solution.py:244
  58.5 0.0 collective-permute-done.4
  58.5 1.2 %collective-permute-done.5 = bf16[256,256]{1,0:T(8,128)(2,1)S(1)} collective-permute-done((bf16[256,256]{1,0:T(8,128)(2,1)S(1)}, bf16[256,256]{1,0:T(8,128)(2,1)S(1)}, u32[]{:S(2)}, u32[]{:S(2)}) %collective-permute-start.5) | collective-permute-done | bytes 131104 | tf_op jit(solution)/shard_map/ppermute | solution.py:244
  59.6 6.3 %collective-permute-done.6 = bf16[256,256]{1,0:T(8,128)(2,1)S(1)} collective-permute-done((bf16[256,256]{1,0:T(8,128)(2,1)S(1)}, bf16[256,256]{1,0:T(8,128)(2,1)S(1)}, u32[]{:S(2)}, u32[]{:S(2)}) %collective-permute-start.6) | collective-permute-done | bytes 131104 | tf_op jit(solution)/shard_map/ppermute | solution.py:244
  65.9 1.9 %collective-permute-done.7 = bf16[256,256]{1,0:T(8,128)(2,1)S(1)} collective-permute-done((bf16[256,256]{1,0:T(8,128)(2,1)S(1)}, bf16[256,256]{1,0:T(8,128)(2,1)S(1)}, u32[]{:S(2)}, u32[]{:S(2)}) %collective-permute-start.7) | collective-permute-done | bytes 131104 | tf_op jit(solution)/shard_map/ppermute | solution.py:244
  67.8 0.7 add_convert_fusion
  68.5 4.4 %all-to-all-start.3 = ((bf16[8,32,256]{2,1,0:T(8,128)(2,1)}), bf16[8,32,256]{2,1,0:T(8,128)(2,1)S(1)}, u32[]{:S(2)}, u32[]{:S(2)}) async-start(bf16[8,32,256]{2,1,0:T(8,128)(2,1)} %bitcast.4), calls=%async_computation.3 | async-start | bytes 262144 | tf_op jit(solution)/shard_map/all_to_all | solution.py:232
  73.0 1.9 %unpack_queries.1 = bf16[32,8192]{1,0:T(8,128)(2,1)} custom-call(bf16[8,32,1024]{2,1,0:T(8,128)(2,1)} %copy-done), custom_call_target="tpu_custom_call" | custom-call | tf_op jit(solution)/shard_map/unpack_queries/pallas_call | solution.py:204
  74.9 4.3 %all-to-all-done.3 = bf16[8,32,256]{2,1,0:T(8,128)(2,1)S(1)} async-done(((bf16[8,32,256]{2,1,0:T(8,128)(2,1)}), bf16[8,32,256]{2,1,0:T(8,128)(2,1)S(1)}, u32[]{:S(2)}, u32[]{:S(2)}) %all-to-all-start.3) | async-done | bytes 131104 | tf_op jit(solution)/shard_map/all_to_all | solution.py:232
  79.1 0.7 copy_bitcast_fusion
  (6 shorter events, 0.0 us)
Async XLA Ops:
  2.2 10.4 %all-to-all-start.1 = ((bf16[8,32,256]{2,1,0:T(8,128)(2,1)}), bf16[8,32,256]{2,1,0:T(8,128)(2,1)S(1)}, u32[]{:S(2)}, u32[]{:S(2)}) async-start(bf16[8,32,256]{2,1,0:T(8,128)(2,1)} %pack_keys.1), calls=%async_computation.1 | async-start | bytes 262144 | tf_op jit(solution)/shard_map/all_to_all | solution.py:232
  9.3 6.9 %copy-start.1 = (s32[16384]{0:T(1024)S(1)}, s32[16384]{0:T(1024)}, u32[]{:S(2)}) copy-start(s32[16384]{0:T(1024)} %param.11) | copy-start | bytes 196612
  12.6 22.1 %all-to-all-start = ((bf16[8,32,2176]{2,1,0:T(8,128)(2,1)}), bf16[8,32,2176]{2,1,0:T(8,128)(2,1)S(1)}, u32[]{:S(2)}, u32[]{:S(2)}) async-start(bf16[8,32,2176]{2,1,0:T(8,128)(2,1)} %pack_queries.1), calls=%async_computation | async-start | bytes 2228224 | tf_op jit(solution)/shard_map/all_to_all | solution.py:232
  16.3 14.7 %collective-permute-start.3 = (bf16[256,256]{1,0:T(8,128)(2,1)S(1)}, bf16[256,256]{1,0:T(8,128)(2,1)S(1)}, u32[]{:S(2)}, u32[]{:S(2)}) collective-permute-start(bf16[256,256]{1,0:T(8,128)(2,1)S(1)} %bitcast.15), channel_id=1, source_target_pairs={{0,8},{1,9},{2,10},{3,11},{4,12},{5,13},{6,14},{7,15},{8,16},{9,17... | collective-permute-start | bytes 393224 | tf_op jit(solution)/shard_map/ppermute | solution.py:244
  21.0 11.8 %collective-permute-start.2 = (bf16[256,256]{1,0:T(8,128)(2,1)S(1)}, bf16[256,256]{1,0:T(8,128)(2,1)S(1)}, u32[]{:S(2)}, u32[]{:S(2)}) collective-permute-start(bf16[256,256]{1,0:T(8,128)(2,1)S(1)} %bitcast.16), channel_id=1, source_target_pairs={{0,16},{1,17},{2,18},{3,19},{4,20},{5,21},{6,22},{7,23},{8,24},{9,... | collective-permute-start | bytes 393224 | tf_op jit(solution)/shard_map/ppermute | solution.py:244
  25.5 8.6 %collective-permute-start.1 = (bf16[256,256]{1,0:T(8,128)(2,1)S(1)}, bf16[256,256]{1,0:T(8,128)(2,1)S(1)}, u32[]{:S(2)}, u32[]{:S(2)}) collective-permute-start(bf16[256,256]{1,0:T(8,128)(2,1)S(1)} %bitcast.17), channel_id=1, source_target_pairs={{0,24},{1,25},{2,26},{3,27},{4,28},{5,29},{6,30},{7,31},{8,32},{9,... | collective-permute-start | bytes 393224 | tf_op jit(solution)/shard_map/ppermute | solution.py:244
  27.7 7.0 %collective-permute-start = (bf16[256,256]{1,0:T(8,128)(2,1)S(1)}, bf16[256,256]{1,0:T(8,128)(2,1)S(1)}, u32[]{:S(2)}, u32[]{:S(2)}) collective-permute-start(bf16[256,256]{1,0:T(8,128)(2,1)S(1)} %bitcast.18), channel_id=1, source_target_pairs={{0,32},{1,33},{2,34},{3,35},{4,36},{5,37},{6,38},{7,39},{8,40},{9,... | collective-permute-start | bytes 393224 | tf_op jit(solution)/shard_map/ppermute | solution.py:244
  42.4 26.1 %all-to-all-start.2 = ((bf16[8,32,1024]{2,1,0:T(8,128)(2,1)}), bf16[8,32,1024]{2,1,0:T(8,128)(2,1)S(1)}, u32[]{:S(2)}, u32[]{:S(2)}) async-start(bf16[8,32,1024]{2,1,0:T(8,128)(2,1)} %bitcast.3), calls=%async_computation.2 | async-start | bytes 1048576 | tf_op jit(solution)/shard_map/all_to_all | solution.py:232
  47.0 11.5 %collective-permute-start.4 = (bf16[256,256]{1,0:T(8,128)(2,1)S(1)}, bf16[256,256]{1,0:T(8,128)(2,1)S(1)}, u32[]{:S(2)}, u32[]{:S(2)}) collective-permute-start(bf16[256,256]{1,0:T(8,128)(2,1)S(1)} %get-tuple-element.12), channel_id=1, source_target_pairs={{32,0},{33,1},{34,2},{35,3},{36,4},{37,5},{38,6},{39,7},{40,8},{41... | collective-permute-start | bytes 393224 | tf_op jit(solution)/shard_map/ppermute | solution.py:244
  49.9 9.7 %collective-permute-start.5 = (bf16[256,256]{1,0:T(8,128)(2,1)S(1)}, bf16[256,256]{1,0:T(8,128)(2,1)S(1)}, u32[]{:S(2)}, u32[]{:S(2)}) collective-permute-start(bf16[256,256]{1,0:T(8,128)(2,1)S(1)} %get-tuple-element.13), channel_id=1, source_target_pairs={{24,0},{25,1},{26,2},{27,3},{28,4},{29,5},{30,6},{31,7},{32,8},{33... | collective-permute-start | bytes 393224 | tf_op jit(solution)/shard_map/ppermute | solution.py:244
  53.8 12.2 %collective-permute-start.6 = (bf16[256,256]{1,0:T(8,128)(2,1)S(1)}, bf16[256,256]{1,0:T(8,128)(2,1)S(1)}, u32[]{:S(2)}, u32[]{:S(2)}) collective-permute-start(bf16[256,256]{1,0:T(8,128)(2,1)S(1)} %get-tuple-element.14), channel_id=1, source_target_pairs={{16,0},{17,1},{18,2},{19,3},{20,4},{21,5},{22,6},{23,7},{24,8},{25... | collective-permute-start | bytes 393224 | tf_op jit(solution)/shard_map/ppermute | solution.py:244
  56.3 11.5 %collective-permute-start.7 = (bf16[256,256]{1,0:T(8,128)(2,1)S(1)}, bf16[256,256]{1,0:T(8,128)(2,1)S(1)}, u32[]{:S(2)}, u32[]{:S(2)}) collective-permute-start(bf16[256,256]{1,0:T(8,128)(2,1)S(1)} %get-tuple-element.15), channel_id=1, source_target_pairs={{8,0},{9,1},{10,2},{11,3},{12,4},{13,5},{14,6},{15,7},{16,8},{17,9... | collective-permute-start | bytes 393224 | tf_op jit(solution)/shard_map/ppermute | solution.py:244
  68.5 4.5 %copy-start = (bf16[8,32,1024]{2,1,0:T(8,128)(2,1)}, bf16[8,32,1024]{2,1,0:T(8,128)(2,1)S(1)}, u32[]{:S(2)}) copy-start(bf16[8,32,1024]{2,1,0:T(8,128)(2,1)S(1)} %all-to-all-done.2.in_ref) | copy-start | bytes 1572868
  68.5 10.6 %all-to-all-start.3 = ((bf16[8,32,256]{2,1,0:T(8,128)(2,1)}), bf16[8,32,256]{2,1,0:T(8,128)(2,1)S(1)}, u32[]{:S(2)}, u32[]{:S(2)}) async-start(bf16[8,32,256]{2,1,0:T(8,128)(2,1)} %bitcast.4), calls=%async_computation.3 | async-start | bytes 262144 | tf_op jit(solution)/shard_map/all_to_all | solution.py:232

commit v5 on v4

--- a/solution.py
+++ b/solution.py
@@ -255,7 +255,7 @@
     kv = [shift(own, steps) for steps in range(BEHIND, 0, -1)] + [own]
     grad_query, *grad_kv = attend(packed, kv, first)
     grad_rows = exchange(grad_query.reshape(sharers, rows, COLUMNS))
-    others = [shift(grad_kv[j], j - BEHIND) for j in range(BEHIND)]
+    others = [shift(grad_kv[BEHIND - steps], -steps) for steps in (3, 2, 4, 1)]
     grad_own = add_parts(grad_kv[BEHIND], others)
     grad_own, grad_rows = lax.optimization_barrier((grad_own, grad_rows))
     kv_rows = exchange(grad_own.reshape(sharers, rows, 2 * HEAD_SIZE))

time: 80.6 us -> 80 us (level)
  transfers between devices with their start and end apart: 12 -> 12, of which waited for: 8 -> 7; matrix products, arithmetic and copies ran while one was open for 1% -> 1% of each run, Pallas kernels for 6% -> 6%
where the time goes in v5:
time: 80 us; the launch traced here: 79.3 us
  starting transfers between devices  42.6 us (53%)
  waiting for transfers between devices  20 us (25%)
  Pallas kernels  14 us (18%)
  other arithmetic  0.97 us (1%)
  local copies, waits for them, and re-layouts  0.86 us (1%)
    ppermute x8, starting transfers between devices, shift(): return lax.ppermute(value, ('ctx', 'head'), pairs)  25.8 us
    all_to_all x4, starting transfers between devices, exchange(): lax.all_to_all(value, 'head', split_axis=0, concat_axis=0, axis_index_gro...  16.9 us
    ppermute x8, waiting for transfers between devices, shift(): return lax.ppermute(value, ('ctx', 'head'), pairs)  12.5 us
    pallas_call x1, Pallas kernels, attend(): pl.pallas_call(attend_kernel, out_shape=[jax.ShapeDtypeStruct((block, COL...  7.73 us
    all_to_all x4, waiting for transfers between devices, exchange(): lax.all_to_all(value, 'head', split_axis=0, concat_axis=0, axis_index_gro...  7.56 us
    pallas_call x1, Pallas kernels, pack_queries(): pl.pallas_call(pack_queries_kernel, out_shape=jax.ShapeDtypeStruct((KEY_V...  2.83 us
    pallas_call x1, Pallas kernels, unpack_queries(): pl.pallas_call(unpack_queries_kernel, out_shape=jax.ShapeDtypeStruct((row...  1.87 us
  transfers between devices with their start and end apart: 12, of which 7 were waited for; matrix products, arithmetic and copies ran while one was open for 1% of the time, Pallas kernels for 6%

profile of v5, /device:TPU:248, one launch (start us, length us, event | category | flops | bytes accessed | tf_op | source)
XLA Modules:
  0.0 79.3 jit_solution(11684417143421643430)
XLA Ops:
  0.6 1.6 %pack_keys.1 = bf16[8,32,256]{2,1,0:T(8,128)(2,1)} custom-call(bf16[32,1024]{1,0:T(8,128)(2,1)} %key_ref.1, bf16[32,1024]{1,0:T(8,128)(2,1)} %value_ref.1), custom_call_target="tpu_custom_call" | custom-call | tf_op jit(solution)/shard_map/pack_keys/pallas_call | solution.py:40
  2.2 4.3 %all-to-all-start.1 = ((bf16[8,32,256]{2,1,0:T(8,128)(2,1)}), bf16[8,32,256]{2,1,0:T(8,128)(2,1)S(1)}, u32[]{:S(2)}, u32[]{:S(2)}) async-start(bf16[8,32,256]{2,1,0:T(8,128)(2,1)} %pack_keys.1), calls=%async_computation.1 | async-start | bytes 262144 | tf_op jit(solution)/shard_map/all_to_all | solution.py:232
  6.5 2.8 %pack_queries.1 = bf16[8,32,2176]{2,1,0:T(8,128)(2,1)} custom-call(bf16[32,8192]{1,0:T(8,128)(2,1)} %query_ref.1, bf16[32,8192]{1,0:T(8,128)(2,1)} %out_ref.1, bf16[32,8192]{1,0:T(8,128)(2,1)} %grad_ref.1), custom_call_target="tpu_custom_call" | custom-call | tf_op jit(solution)/shard_map/pack_queries/pallas_call | solution.py:75
  9.3 3.3 %all-to-all-done.1 = bf16[8,32,256]{2,1,0:T(8,128)(2,1)S(1)} async-done(((bf16[8,32,256]{2,1,0:T(8,128)(2,1)}), bf16[8,32,256]{2,1,0:T(8,128)(2,1)S(1)}, u32[]{:S(2)}, u32[]{:S(2)}) %all-to-all-start.1) | async-done | bytes 131104 | tf_op jit(solution)/shard_map/all_to_all | solution.py:232
  12.6 3.6 %all-to-all-start = ((bf16[8,32,2176]{2,1,0:T(8,128)(2,1)}), bf16[8,32,2176]{2,1,0:T(8,128)(2,1)S(1)}, u32[]{:S(2)}, u32[]{:S(2)}) async-start(bf16[8,32,2176]{2,1,0:T(8,128)(2,1)} %pack_queries.1), calls=%async_computation | async-start | bytes 2228224 | tf_op jit(solution)/shard_map/all_to_all | solution.py:232
  16.2 0.1 pad_dynamic-slice_fusion.1
  16.3 4.7 %collective-permute-start.3 = (bf16[256,256]{1,0:T(8,128)(2,1)S(1)}, bf16[256,256]{1,0:T(8,128)(2,1)S(1)}, u32[]{:S(2)}, u32[]{:S(2)}) collective-permute-start(bf16[256,256]{1,0:T(8,128)(2,1)S(1)} %bitcast.15), channel_id=1, source_target_pairs={{0,8},{1,9},{2,10},{3,11},{4,12},{5,13},{6,14},{7,15},{8,16},{9,17... | collective-permute-start | bytes 393224 | tf_op jit(solution)/shard_map/ppermute | solution.py:244
  21.0 4.5 %collective-permute-start.2 = (bf16[256,256]{1,0:T(8,128)(2,1)S(1)}, bf16[256,256]{1,0:T(8,128)(2,1)S(1)}, u32[]{:S(2)}, u32[]{:S(2)}) collective-permute-start(bf16[256,256]{1,0:T(8,128)(2,1)S(1)} %bitcast.16), channel_id=1, source_target_pairs={{0,16},{1,17},{2,18},{3,19},{4,20},{5,21},{6,22},{7,23},{8,24},{9,... | collective-permute-start | bytes 393224 | tf_op jit(solution)/shard_map/ppermute | solution.py:244
  25.5 2.2 %collective-permute-start.1 = (bf16[256,256]{1,0:T(8,128)(2,1)S(1)}, bf16[256,256]{1,0:T(8,128)(2,1)S(1)}, u32[]{:S(2)}, u32[]{:S(2)}) collective-permute-start(bf16[256,256]{1,0:T(8,128)(2,1)S(1)} %bitcast.17), channel_id=1, source_target_pairs={{0,24},{1,25},{2,26},{3,27},{4,28},{5,29},{6,30},{7,31},{8,32},{9,... | collective-permute-start | bytes 393224 | tf_op jit(solution)/shard_map/ppermute | solution.py:244
  27.7 2.9 %collective-permute-start = (bf16[256,256]{1,0:T(8,128)(2,1)S(1)}, bf16[256,256]{1,0:T(8,128)(2,1)S(1)}, u32[]{:S(2)}, u32[]{:S(2)}) collective-permute-start(bf16[256,256]{1,0:T(8,128)(2,1)S(1)} %bitcast.18), channel_id=1, source_target_pairs={{0,32},{1,33},{2,34},{3,35},{4,36},{5,37},{6,38},{7,39},{8,40},{9,... | collective-permute-start | bytes 393224 | tf_op jit(solution)/shard_map/ppermute | solution.py:244
  30.7 0.1 pad_dynamic-slice_fusion
  30.7 0.2 convert_reduce_fusion
  31.0 0.0 collective-permute-done.3.kv3
  31.0 1.8 %collective-permute-done.2.kv2 = bf16[256,256]{1,0:T(8,128)(2,1)S(1)} collective-permute-done((bf16[256,256]{1,0:T(8,128)(2,1)S(1)}, bf16[256,256]{1,0:T(8,128)(2,1)S(1)}, u32[]{:S(2)}, u32[]{:S(2)}) %collective-permute-start.2) | collective-permute-done | bytes 131104 | tf_op jit(solution)/shard_map/ppermute | solution.py:244
  32.8 1.3 %collective-permute-done.1.kv1 = bf16[256,256]{1,0:T(8,128)(2,1)S(1)} collective-permute-done((bf16[256,256]{1,0:T(8,128)(2,1)S(1)}, bf16[256,256]{1,0:T(8,128)(2,1)S(1)}, u32[]{:S(2)}, u32[]{:S(2)}) %collective-permute-start.1) | collective-permute-done | bytes 131104 | tf_op jit(solution)/shard_map/ppermute | solution.py:244
  34.1 0.5 collective-permute-done.kv0
  34.7 0.0 all-to-all-done
  34.7 7.7 %attend.1 = (bf16[256,1024]{1,0:T(8,128)(2,1)}, bf16[256,256]{1,0:T(8,128)(2,1)S(1)}, bf16[256,256]{1,0:T(8,128)(2,1)S(1)}, bf16[256,256]{1,0:T(8,128)(2,1)S(1)}...) custom-call(bf16[256,2176]{1,0:T(8,128)(2,1)S(1)} %bitcast.14, bf16[256,256]{1,0:T(8,128)(2,1)S(1)} %collective-permute-done.kv0, ...), custom_call_target="tpu_custom_call" | custom-call | tf_op jit(solution)/shard_map/attend/pallas_call | solution.py:171
  42.4 4.6 %all-to-all-start.2 = ((bf16[8,32,1024]{2,1,0:T(8,128)(2,1)}), bf16[8,32,1024]{2,1,0:T(8,128)(2,1)S(1)}, u32[]{:S(2)}, u32[]{:S(2)}) async-start(bf16[8,32,1024]{2,1,0:T(8,128)(2,1)} %bitcast.3), calls=%async_computation.2 | async-start | bytes 1048576 | tf_op jit(solution)/shard_map/all_to_all | solution.py:232
  47.0 4.8 %collective-permute-start.4 = (bf16[256,256]{1,0:T(8,128)(2,1)S(1)}, bf16[256,256]{1,0:T(8,128)(2,1)S(1)}, u32[]{:S(2)}, u32[]{:S(2)}) collective-permute-start(bf16[256,256]{1,0:T(8,128)(2,1)S(1)} %get-tuple-element.12), channel_id=1, source_target_pairs={{24,0},{25,1},{26,2},{27,3},{28,4},{29,5},{30,6},{31,7},{32,8},{33... | collective-permute-start | bytes 393224 | tf_op jit(solution)/shard_map/ppermute | solution.py:244
  51.8 2.5 %collective-permute-start.5 = (bf16[256,256]{1,0:T(8,128)(2,1)S(1)}, bf16[256,256]{1,0:T(8,128)(2,1)S(1)}, u32[]{:S(2)}, u32[]{:S(2)}) collective-permute-start(bf16[256,256]{1,0:T(8,128)(2,1)S(1)} %get-tuple-element.13), channel_id=1, source_target_pairs={{16,0},{17,1},{18,2},{19,3},{20,4},{21,5},{22,6},{23,7},{24,8},{25... | collective-permute-start | bytes 393224 | tf_op jit(solution)/shard_map/ppermute | solution.py:244
  54.4 1.9 %collective-permute-start.6 = (bf16[256,256]{1,0:T(8,128)(2,1)S(1)}, bf16[256,256]{1,0:T(8,128)(2,1)S(1)}, u32[]{:S(2)}, u32[]{:S(2)}) collective-permute-start(bf16[256,256]{1,0:T(8,128)(2,1)S(1)} %get-tuple-element.14), channel_id=1, source_target_pairs={{32,0},{33,1},{34,2},{35,3},{36,4},{37,5},{38,6},{39,7},{40,8},{41... | collective-permute-start | bytes 393224 | tf_op jit(solution)/shard_map/ppermute | solution.py:244
  56.3 2.2 %collective-permute-start.7 = (bf16[256,256]{1,0:T(8,128)(2,1)S(1)}, bf16[256,256]{1,0:T(8,128)(2,1)S(1)}, u32[]{:S(2)}, u32[]{:S(2)}) collective-permute-start(bf16[256,256]{1,0:T(8,128)(2,1)S(1)} %get-tuple-element.15), channel_id=1, source_target_pairs={{8,0},{9,1},{10,2},{11,3},{12,4},{13,5},{14,6},{15,7},{16,8},{17,9... | collective-permute-start | bytes 393224 | tf_op jit(solution)/shard_map/ppermute | solution.py:244
  58.5 0.0 collective-permute-done.4
  58.5 5.2 %collective-permute-done.5 = bf16[256,256]{1,0:T(8,128)(2,1)S(1)} collective-permute-done((bf16[256,256]{1,0:T(8,128)(2,1)S(1)}, bf16[256,256]{1,0:T(8,128)(2,1)S(1)}, u32[]{:S(2)}, u32[]{:S(2)}) %collective-permute-start.5) | collective-permute-done | bytes 131104 | tf_op jit(solution)/shard_map/ppermute | solution.py:244
  63.7 0.0 collective-permute-done.6
  63.7 3.6 %collective-permute-done.7 = bf16[256,256]{1,0:T(8,128)(2,1)S(1)} collective-permute-done((bf16[256,256]{1,0:T(8,128)(2,1)S(1)}, bf16[256,256]{1,0:T(8,128)(2,1)S(1)}, u32[]{:S(2)}, u32[]{:S(2)}) %collective-permute-start.7) | collective-permute-done | bytes 131104 | tf_op jit(solution)/shard_map/ppermute | solution.py:244
  67.3 0.7 add_convert_fusion
  68.0 4.4 %all-to-all-start.3 = ((bf16[8,32,256]{2,1,0:T(8,128)(2,1)}), bf16[8,32,256]{2,1,0:T(8,128)(2,1)S(1)}, u32[]{:S(2)}, u32[]{:S(2)}) async-start(bf16[8,32,256]{2,1,0:T(8,128)(2,1)} %bitcast.4), calls=%async_computation.3 | async-start | bytes 262144 | tf_op jit(solution)/shard_map/all_to_all | solution.py:232
  72.4 1.9 %unpack_queries.1 = bf16[32,8192]{1,0:T(8,128)(2,1)} custom-call(bf16[8,32,1024]{2,1,0:T(8,128)(2,1)} %copy-done), custom_call_target="tpu_custom_call" | custom-call | tf_op jit(solution)/shard_map/unpack_queries/pallas_call | solution.py:204
  74.3 4.3 %all-to-all-done.3 = bf16[8,32,256]{2,1,0:T(8,128)(2,1)S(1)} async-done(((bf16[8,32,256]{2,1,0:T(8,128)(2,1)}), bf16[8,32,256]{2,1,0:T(8,128)(2,1)S(1)}, u32[]{:S(2)}, u32[]{:S(2)}) %all-to-all-start.3) | async-done | bytes 131104 | tf_op jit(solution)/shard_map/all_to_all | solution.py:232
  78.6 0.7 copy_bitcast_fusion
  (6 shorter events, 0.0 us)
Async XLA Ops:
  2.2 10.4 %all-to-all-start.1 = ((bf16[8,32,256]{2,1,0:T(8,128)(2,1)}), bf16[8,32,256]{2,1,0:T(8,128)(2,1)S(1)}, u32[]{:S(2)}, u32[]{:S(2)}) async-start(bf16[8,32,256]{2,1,0:T(8,128)(2,1)} %pack_keys.1), calls=%async_computation.1 | async-start | bytes 262144 | tf_op jit(solution)/shard_map/all_to_all | solution.py:232
  9.3 6.9 %copy-start.1 = (s32[16384]{0:T(1024)S(1)}, s32[16384]{0:T(1024)}, u32[]{:S(2)}) copy-start(s32[16384]{0:T(1024)} %param.11) | copy-start | bytes 196612
  12.6 22.1 %all-to-all-start = ((bf16[8,32,2176]{2,1,0:T(8,128)(2,1)}), bf16[8,32,2176]{2,1,0:T(8,128)(2,1)S(1)}, u32[]{:S(2)}, u32[]{:S(2)}) async-start(bf16[8,32,2176]{2,1,0:T(8,128)(2,1)} %pack_queries.1), calls=%async_computation | async-start | bytes 2228224 | tf_op jit(solution)/shard_map/all_to_all | solution.py:232
  16.3 14.7 %collective-permute-start.3 = (bf16[256,256]{1,0:T(8,128)(2,1)S(1)}, bf16[256,256]{1,0:T(8,128)(2,1)S(1)}, u32[]{:S(2)}, u32[]{:S(2)}) collective-permute-start(bf16[256,256]{1,0:T(8,128)(2,1)S(1)} %bitcast.15), channel_id=1, source_target_pairs={{0,8},{1,9},{2,10},{3,11},{4,12},{5,13},{6,14},{7,15},{8,16},{9,17... | collective-permute-start | bytes 393224 | tf_op jit(solution)/shard_map/ppermute | solution.py:244
  21.0 11.8 %collective-permute-start.2 = (bf16[256,256]{1,0:T(8,128)(2,1)S(1)}, bf16[256,256]{1,0:T(8,128)(2,1)S(1)}, u32[]{:S(2)}, u32[]{:S(2)}) collective-permute-start(bf16[256,256]{1,0:T(8,128)(2,1)S(1)} %bitcast.16), channel_id=1, source_target_pairs={{0,16},{1,17},{2,18},{3,19},{4,20},{5,21},{6,22},{7,23},{8,24},{9,... | collective-permute-start | bytes 393224 | tf_op jit(solution)/shard_map/ppermute | solution.py:244
  25.5 8.6 %collective-permute-start.1 = (bf16[256,256]{1,0:T(8,128)(2,1)S(1)}, bf16[256,256]{1,0:T(8,128)(2,1)S(1)}, u32[]{:S(2)}, u32[]{:S(2)}) collective-permute-start(bf16[256,256]{1,0:T(8,128)(2,1)S(1)} %bitcast.17), channel_id=1, source_target_pairs={{0,24},{1,25},{2,26},{3,27},{4,28},{5,29},{6,30},{7,31},{8,32},{9,... | collective-permute-start | bytes 393224 | tf_op jit(solution)/shard_map/ppermute | solution.py:244
  27.7 7.0 %collective-permute-start = (bf16[256,256]{1,0:T(8,128)(2,1)S(1)}, bf16[256,256]{1,0:T(8,128)(2,1)S(1)}, u32[]{:S(2)}, u32[]{:S(2)}) collective-permute-start(bf16[256,256]{1,0:T(8,128)(2,1)S(1)} %bitcast.18), channel_id=1, source_target_pairs={{0,32},{1,33},{2,34},{3,35},{4,36},{5,37},{6,38},{7,39},{8,40},{9,... | collective-permute-start | bytes 393224 | tf_op jit(solution)/shard_map/ppermute | solution.py:244
  42.4 25.6 %all-to-all-start.2 = ((bf16[8,32,1024]{2,1,0:T(8,128)(2,1)}), bf16[8,32,1024]{2,1,0:T(8,128)(2,1)S(1)}, u32[]{:S(2)}, u32[]{:S(2)}) async-start(bf16[8,32,1024]{2,1,0:T(8,128)(2,1)} %bitcast.3), calls=%async_computation.2 | async-start | bytes 1048576 | tf_op jit(solution)/shard_map/all_to_all | solution.py:232
  47.0 11.5 %collective-permute-start.4 = (bf16[256,256]{1,0:T(8,128)(2,1)S(1)}, bf16[256,256]{1,0:T(8,128)(2,1)S(1)}, u32[]{:S(2)}, u32[]{:S(2)}) collective-permute-start(bf16[256,256]{1,0:T(8,128)(2,1)S(1)} %get-tuple-element.12), channel_id=1, source_target_pairs={{24,0},{25,1},{26,2},{27,3},{28,4},{29,5},{30,6},{31,7},{32,8},{33... | collective-permute-start | bytes 393224 | tf_op jit(solution)/shard_map/ppermute | solution.py:244
  51.8 11.8 %collective-permute-start.5 = (bf16[256,256]{1,0:T(8,128)(2,1)S(1)}, bf16[256,256]{1,0:T(8,128)(2,1)S(1)}, u32[]{:S(2)}, u32[]{:S(2)}) collective-permute-start(bf16[256,256]{1,0:T(8,128)(2,1)S(1)} %get-tuple-element.13), channel_id=1, source_target_pairs={{16,0},{17,1},{18,2},{19,3},{20,4},{21,5},{22,6},{23,7},{24,8},{25... | collective-permute-start | bytes 393224 | tf_op jit(solution)/shard_map/ppermute | solution.py:244
  54.4 9.3 %collective-permute-start.6 = (bf16[256,256]{1,0:T(8,128)(2,1)S(1)}, bf16[256,256]{1,0:T(8,128)(2,1)S(1)}, u32[]{:S(2)}, u32[]{:S(2)}) collective-permute-start(bf16[256,256]{1,0:T(8,128)(2,1)S(1)} %get-tuple-element.14), channel_id=1, source_target_pairs={{32,0},{33,1},{34,2},{35,3},{36,4},{37,5},{38,6},{39,7},{40,8},{41... | collective-permute-start | bytes 393224 | tf_op jit(solution)/shard_map/ppermute | solution.py:244
  56.3 11.0 %collective-permute-start.7 = (bf16[256,256]{1,0:T(8,128)(2,1)S(1)}, bf16[256,256]{1,0:T(8,128)(2,1)S(1)}, u32[]{:S(2)}, u32[]{:S(2)}) collective-permute-start(bf16[256,256]{1,0:T(8,128)(2,1)S(1)} %get-tuple-element.15), channel_id=1, source_target_pairs={{8,0},{9,1},{10,2},{11,3},{12,4},{13,5},{14,6},{15,7},{16,8},{17,9... | collective-permute-start | bytes 393224 | tf_op jit(solution)/shard_map/ppermute | solution.py:244
  68.0 4.5 %copy-start = (bf16[8,32,1024]{2,1,0:T(8,128)(2,1)}, bf16[8,32,1024]{2,1,0:T(8,128)(2,1)S(1)}, u32[]{:S(2)}) copy-start(bf16[8,32,1024]{2,1,0:T(8,128)(2,1)S(1)} %all-to-all-done.2.in_ref) | copy-start | bytes 1572868
  68.0 10.6 %all-to-all-start.3 = ((bf16[8,32,256]{2,1,0:T(8,128)(2,1)}), bf16[8,32,256]{2,1,0:T(8,128)(2,1)S(1)}, u32[]{:S(2)}, u32[]{:S(2)}) async-start(bf16[8,32,256]{2,1,0:T(8,128)(2,1)} %bitcast.4), calls=%async_computation.3 | async-start | bytes 262144 | tf_op jit(solution)/shard_map/all_to_all | solution.py:232
